TPU v7x, 128 devices: a whole 4x4x4 slice. The times are simulated.
128 devices in a mesh: dp: 32 (over y, z, core), tensor: 4 (over x).
Axes of the slice: x: 4, y: 4, z: 4, core: 2. Of those that a mesh axis runs over, the one named last changes fastest.
Arguments:
- tokens: bfloat16 [4096, 4096], P('dp', 'tensor'), may hold values from -6 to 6
- cotangent: bfloat16 [4096, 4096], P('dp', 'tensor'), may hold values from -6 to 6
- expert_ids: int32 [4096, 8], P('dp'), may hold values from 0 to 63, all different within a row; in each aligned block of 128 rows (0 to 127, 128 to 255, ...) at most 20 rows name the same one
- gates: bfloat16 [4096, 8], P('dp'), may hold values from 0.029907227 to 0.59765625
- w_gate: bfloat16 [64, 4096, 1024], P('dp', None, 'tensor'), may hold values from -0.09375 to 0.09375
- w_up: bfloat16 [64, 4096, 1024], P('dp', None, 'tensor'), may hold values from -0.09375 to 0.09375
- w_down: bfloat16 [64, 1024, 4096], P('dp', 'tensor'), may hold values from -0.1875 to 0.1875
Outputs:
- grad_tokens: bfloat16 [4096, 4096], P('dp', 'tensor')
- grad_gates: bfloat16 [4096, 8], P('dp')
- grad_w_gate: bfloat16 [64, 4096, 1024], P('dp', None, 'tensor')
- grad_w_up: bfloat16 [64, 4096, 1024], P('dp', None, 'tensor')
- grad_w_down: bfloat16 [64, 1024, 4096], P('dp', 'tensor')
Inputs may be any that keep to these rules, and one draw needn't show every extreme that they name: `expert_ids`: each token names 8 different experts. Among the tokens of one block of 128, no expert is named more than 20 times, and in every draw some expert is named exactly 20 times in some block.
All inputs are finite; a program needn't handle non-finite values.
Results may differ from a plain program's by a relative error of at most 0.015.
Values may be sent and summed in bfloat16 or wider, within the bound.
No kernel may reach another device: no remote copies, remote signals or barrier semaphores. Data moves between devices by JAX's collectives and lax.ppermute only.
A program may use at most 256 MiB of HBM per device.

v0:
```python
import jax
import jax.numpy as jnp
from jax import lax
from jax.sharding import PartitionSpec as P


def place_rows(values, position, total_rows):
    shape_rest = values.shape[1:]
    return jnp.zeros((total_rows,) + shape_rest, values.dtype).at[position].set(values)


def body(tokens, cotangent, expert_ids, gates, w_gate, w_up, w_down):
    tok_count = tokens.shape[0]
    route_top = expert_ids.shape[1]
    local_experts = w_gate.shape[0]
    model_width = w_gate.shape[1]
    dp_count = lax.axis_size("dp")
    experts = local_experts * dp_count
    capacity = max(2, tok_count * route_top * 5 // (4 * experts))
    flat_ids = expert_ids.reshape(-1)
    onehot = (flat_ids[:, None] == jnp.arange(experts, dtype=jnp.int32)[None, :]).astype(jnp.int32)
    before = jnp.cumsum(onehot, axis=0) - onehot
    slot = jnp.sum(before * onehot, axis=1)
    position = flat_ids * capacity + slot
    total_rows = experts * capacity
    g_send = place_rows(gates.reshape(-1), position, total_rows).reshape(experts, capacity)
    full_x, full_dy = (
        lax.all_gather(tokens, "tensor", axis=1, tiled=True),
        lax.all_gather(cotangent, "tensor", axis=1, tiled=True),
    )
    x_send = place_rows(jnp.repeat(full_x, route_top, axis=0), position, total_rows).reshape(
        experts, capacity, model_width
    )
    dy_send = place_rows(jnp.repeat(full_dy, route_top, axis=0), position, total_rows).reshape(
        experts, capacity, model_width
    )
    x_rows, dy_rows, g_rows = (
        lax.all_to_all(x_send, "dp", split_axis=0, concat_axis=1, tiled=True),
        lax.all_to_all(dy_send, "dp", split_axis=0, concat_axis=1, tiled=True),
        lax.all_to_all(g_send, "dp", split_axis=0, concat_axis=1, tiled=True),
    )
    h_one = jnp.einsum("erd,edf->erf", x_rows, w_gate, preferred_element_type=jnp.float32)
    h_two = jnp.einsum("erd,edf->erf", x_rows, w_up, preferred_element_type=jnp.float32)
    sigmoid_gate = jax.nn.sigmoid(h_one)
    act = (h_one * sigmoid_gate * h_two).astype(jnp.bfloat16)
    out_part = jnp.einsum("erf,efd->erd", act, w_down, preferred_element_type=jnp.float32)
    route_terms = jnp.sum(out_part * dy_rows.astype(jnp.float32), axis=2)
    grad_route = lax.psum(route_terms, "tensor").astype(jnp.bfloat16)
    dout = (g_rows.astype(jnp.float32)[:, :, None] * dy_rows.astype(jnp.float32)).astype(
        jnp.bfloat16
    )
    grad_down = jnp.einsum("erf,erd->efd", act, dout, preferred_element_type=jnp.float32).astype(
        jnp.bfloat16
    )
    d_act = jnp.einsum("erd,efd->erf", dout, w_down, preferred_element_type=jnp.float32)
    d_two = (d_act * h_one * sigmoid_gate).astype(jnp.bfloat16)
    d_one = (d_act * h_two * sigmoid_gate * (1.0 + h_one * (1.0 - sigmoid_gate))).astype(
        jnp.bfloat16
    )
    grad_gate = jnp.einsum(
        "erd,erf->edf", x_rows, d_one, preferred_element_type=jnp.float32
    ).astype(jnp.bfloat16)
    grad_up = jnp.einsum("erd,erf->edf", x_rows, d_two, preferred_element_type=jnp.float32).astype(
        jnp.bfloat16
    )
    dx_part = jnp.einsum("erf,edf->erd", d_one, w_gate, preferred_element_type=jnp.float32)
    dx_part = dx_part + jnp.einsum("erf,edf->erd", d_two, w_up, preferred_element_type=jnp.float32)
    dx_share = lax.psum_scatter(
        dx_part.astype(jnp.bfloat16), "tensor", scatter_dimension=2, tiled=True
    )
    share_width = dx_share.shape[2]
    dx_send = dx_share.reshape(local_experts, dp_count, capacity, share_width)
    route_send = grad_route.reshape(local_experts, dp_count, capacity)
    dx_back, route_back = (
        lax.all_to_all(dx_send, "dp", split_axis=1, concat_axis=0, tiled=True),
        lax.all_to_all(route_send, "dp", split_axis=1, concat_axis=0, tiled=True),
    )
    back_rows = dx_back.reshape(total_rows, share_width)[position]
    grad_tokens = jnp.sum(
        back_rows.astype(jnp.float32).reshape(tok_count, route_top, share_width), axis=1
    ).astype(jnp.bfloat16)
    grad_gates = route_back.reshape(total_rows)[position].reshape(tok_count, route_top)
    return (grad_tokens, grad_gates, grad_gate, grad_up, grad_down)


def solution(mesh):
    in_specs = (
        P("dp", "tensor"),
        P("dp", "tensor"),
        P("dp", None),
        P("dp", None),
        P("dp", None, "tensor"),
        P("dp", None, "tensor"),
        P("dp", "tensor", None),
    )
    out_specs = (
        P("dp", "tensor"),
        P("dp", None),
        P("dp", None, "tensor"),
        P("dp", None, "tensor"),
        P("dp", "tensor", None),
    )
    return jax.shard_map(body, mesh=mesh, in_specs=in_specs, out_specs=out_specs, check_vma=False)
```

profile of v0, /device:TPU:1, one launch (start us, length us, event | category | flops | bytes accessed | tf_op | source)
XLA Modules:
  0.0 788.5 jit_solution(18429691845299637836)
XLA Ops:
  10.7 18.0 %reduce-window.6 = s32[64,8,128]{2,1,0:T(8,128)S(1)} reduce-window(s32[64,8,128]{2,1,0:T(8,128)S(1)} %fusion.12, s32[]{:T(128)} %constant.8.clone.1), window={size=1x1x128 pad=0_0x0_0x127_0}, to_apply=%region_0.0 | reduce-window | flops 8323072 | bytes 524292 | tf_op jit(solution)/shard_map/reduce-window
  37.7 9.9 %all-to-all-start = ((bf16[32,2,20]{2,1,0:T(2,128)(2,1)}), bf16[32,2,20]{2,1,0:T(2,128)(2,1)S(1)}, u32[]{:S(2)}, u32[]{:S(2)}) async-start(bf16[32,2,20]{2,1,0:T(2,128)(2,1)} %all_to_all.52), calls=%async_computation | async-start | bytes 32768 | tf_op jit(solution)/shard_map/all_to_all | solution.py:40
  47.6 17.7 %scatter_custom_fusion.2 = bf16[1280,4096]{1,0:T(8,128)(2,1)} fusion(s32[1024]{0:T(1024)S(1)} %bitcast.82, bf16[]{:T(256)} %constant.6.clone.1, bf16[128,4096]{1,0:T(8,128)(2,1)} %all-gather.5.cloned.1.call-done), kind=kCustom, calls=%fused_computation.9 | custom fusion | bytes 11534338 | tf_op jit(solution)/shard_map/scatter | solution.py:9
  65.3 13.8 %reshape.111 = bf16[64,20,4096]{2,1,0:T(8,128)(2,1)} reshape(bf16[1280,4096]{1,0:T(8,128)(2,1)} %scatter_custom_fusion.2) | data formatting | bytes 20971520 | tf_op jit(solution)/shard_map/reshape | solution.py:31
  87.3 25.8 %all-gather.3.cloned.1.call-done = bf16[128,4096]{1,0:T(8,128)(2,1)} async-done(((bf16[128,1024]{1,0:T(8,128)(2,1)}), bf16[128,4096]{1,0:T(8,128)(2,1)}) %all-gather.3.cloned.1.call-update) | async-done | bytes 1048592 | tf_op jit(solution)/shard_map/all_gather | solution.py:29
  113.1 17.7 %scatter_custom_fusion.1 = bf16[1280,4096]{1,0:T(8,128)(2,1)} fusion(s32[1024]{0:T(1024)S(1)} %bitcast.83, bf16[]{:T(256)} %constant.6.clone.1, bf16[128,4096]{1,0:T(8,128)(2,1)} %all-gather.3.cloned.1.call-done), kind=kCustom, calls=%fused_computation.11 | custom fusion | bytes 11534338 | tf_op jit(solution)/shard_map/scatter | solution.py:9
  130.8 13.9 %reshape.109 = bf16[64,20,4096]{2,1,0:T(8,128)(2,1)} reshape(bf16[1280,4096]{1,0:T(8,128)(2,1)} %scatter_custom_fusion.1) | data formatting | bytes 20971520 | tf_op jit(solution)/shard_map/reshape | solution.py:34
  144.7 116.6 %all-to-all-done.2 = bf16[64,20,4096]{2,1,0:T(8,128)(2,1)} async-done(((bf16[64,20,4096]{2,1,0:T(8,128)(2,1)}), bf16[64,20,4096]{2,1,0:T(8,128)(2,1)}, u32[]{:S(2)}, u32[]{:S(2)}) %all-to-all-start.2) | async-done | bytes 10485792 | tf_op jit(solution)/shard_map/all_to_all | solution.py:38
  261.2 29.7 %all-to-all-start.1 = ((bf16[64,20,4096]{2,1,0:T(8,128)(2,1)}), bf16[64,20,4096]{2,1,0:T(8,128)(2,1)}, u32[]{:S(2)}, u32[]{:S(2)}) async-start(bf16[64,20,4096]{2,1,0:T(8,128)(2,1)} %reshape.109), calls=%async_computation.1 | async-start | bytes 25165824 | tf_op jit(solution)/shard_map/all_to_all | solution.py:39
  291.5 19.5 %copy.110 = bf16[32,2,20,4096]{3,1,2,0:T(2,128)(2,1)} copy(bf16[32,2,20,4096]{3,2,1,0:T(8,128)(2,1)} %bitcast.9) | data formatting | bytes 20971520 | tf_op jit(solution)/shard_map/all_to_all | solution.py:38
  310.9 26.4 %copy.104 = bf16[2,640,4096]{1,2,0:T(8,128)(2,1)} copy(bf16[2,640,4096]{2,0,1:T(2,128)(2,1)} %bitcast.73) | data formatting | bytes 20971520 | tf_op jit(solution)/shard_map/all_to_all | solution.py:38
  337.3 128.2 %all-to-all-done.1 = bf16[64,20,4096]{2,1,0:T(8,128)(2,1)} async-done(((bf16[64,20,4096]{2,1,0:T(8,128)(2,1)}), bf16[64,20,4096]{2,1,0:T(8,128)(2,1)}, u32[]{:S(2)}, u32[]{:S(2)}) %all-to-all-start.1) | async-done | bytes 10485792 | tf_op jit(solution)/shard_map/all_to_all | solution.py:39
  465.5 13.6 %copy_convert_fusion = f32[64,20,4096]{2,0,1:T(8,128)} fusion(bf16[64,20,4096]{2,1,0:T(8,128)(2,1)} %all-to-all-done.1), kind=kLoop, calls=%fused_computation.8 | loop fusion | flops 5242880 | bytes 31457280 | tf_op jit(solution)/shard_map/convert_element_type | solution.py:49
  479.2 24.8 %reshape.119 = f32[32,2,20,4096]{3,1,0,2:T(2,128)} reshape(f32[64,20,4096]{2,0,1:T(8,128)} %copy_convert_fusion) | data formatting | bytes 41943040 | tf_op jit(solution)/shard_map/convert_element_type | solution.py:49
  503.9 14.8 %copy.94 = f32[2,32,20,4096]{3,0,2,1:T(2,128)} copy(f32[2,32,20,4096]{3,0,1,2:T(2,128)} %bitcast.72) | data formatting | bytes 41943040 | tf_op jit(solution)/shard_map/convert_element_type | solution.py:49
  518.8 10.5 %fusion.15 = f32[2,640,256]{2,1,0:T(8,128)} fusion(bf16[2,640,4096]{1,2,0:T(8,128)(2,1)} %copy.104, bf16[2,4096,256]{2,1,0:T(8,128)(2,1)} %param.11), kind=kOutput, calls=%fused_computation.40 | convolution fusion | flops 2684354560 | bytes 15990784 | tf_op jit(solution)/shard_map/erd,edf->erf/dot_general | solution.py:42
  529.3 21.3 %fusion.8 = f32[2,640,256]{2,1,0:T(8,128)S(1)} fusion(bf16[2,256,4096]{2,1,0:T(8,128)(2,1)S(1)} %copy-done, f32[2,640,4096]{2,0,1:T(2,128)} %bitcast.69, f32[2,640]{1,0:T(2,128)S(1)} %reshape.117), kind=kOutput, calls=%fused_computation.20 | convolution fusion | flops 2694840320 | bytes 26481664 | tf_op jit(solution)/shard_map/erd,efd->erf/dot_general | solution.py:55
  550.6 10.0 %multiply_convert_fusion.3 = (bf16[2,640,256]{2,1,0:T(8,128)(2,1)S(1)}, bf16[2,640,256]{2,1,0:T(8,128)(2,1)S(1)}, bf16[2,640,256]{2,1,0:T(8,128)(2,1)S(1)}) fusion(f32[2,640,256]{2,1,0:T(8,128)} %fusion.15, f32[2,640,256]{2,1,0:T(8,128)S(1)} %fusion.8, bf16[2,640,4096]{1,2,0:T(8,128)(2,1)} %copy.104, bf16[2,4096,256]{2,1,0:T(8,128)(2,1)} %param.12), kind=kOutput, calls=%fused_computation.22 | convolution fusion | flops 2689597440 | bytes 19267584 | tf_op jit(solution)/shard_map/erd,edf->erf/dot_general | solution.py:43
  560.6 11.0 %fusion.16 = f32[2,640,4096]{2,1,0:T(8,128)} fusion(bf16[2,640,256]{2,1,0:T(8,128)(2,1)S(1)} %get-tuple-element.26, bf16[2,4096,256]{2,1,0:T(8,128)(2,1)} %param.11), kind=kOutput, calls=%fused_computation.41 | convolution fusion | flops 2684354560 | bytes 25821184 | tf_op jit(solution)/shard_map/erf,edf->erd/dot_general | solution.py:66
  571.6 13.4 %add_convert_fusion = bf16[2,640,4096]{2,1,0:T(8,128)(2,1)} fusion(f32[2,640,4096]{2,1,0:T(8,128)} %fusion.16, bf16[2,640,256]{2,1,0:T(8,128)(2,1)S(1)} %get-tuple-element.27, bf16[2,4096,256]{2,1,0:T(8,128)(2,1)} %param.12), kind=kOutput, calls=%fused_computation.6 | convolution fusion | flops 2694840320 | bytes 36306944 | tf_op jit(solution)/shard_map/erf,edf->erd/dot_general | solution.py:67
  585.0 21.0 %multiply_reduce_fusion = f32[2,640]{1,0:T(2,128)S(1)} fusion(f32[2,640,4096]{2,0,1:T(2,128)} %bitcast.70, bf16[2,640,256]{2,1,0:T(8,128)(2,1)S(1)} %get-tuple-element.25, bf16[2,256,4096]{2,1,0:T(8,128)(2,1)} %param.13), kind=kOutput, calls=%fused_computation.5 | convolution fusion | flops 2694839040 | bytes 25826304 | tf_op jit(solution)/shard_map/erf,efd->erd/dot_general | solution.py:46
  615.3 32.3 %all-to-all-start.4 = ((bf16[2,32,20]{2,0,1:T(2,128)(2,1)}), bf16[2,32,20]{2,0,1:T(2,128)(2,1)S(1)}, u32[]{:S(2)}, u32[]{:S(2)}) async-start(bf16[2,32,20]{2,0,1:T(2,128)(2,1)} %copy.103), calls=%async_computation.5 | async-start | bytes 32768 | tf_op jit(solution)/shard_map/all_to_all | solution.py:76
  647.6 58.3 %reduce-scatter.2.cloned.1.call-done = bf16[2,640,1024]{2,1,0:T(8,128)(2,1)} async-done(((bf16[2,640,4096]{2,1,0:T(8,128)(2,1)}), bf16[2,640,1024]{2,1,0:T(8,128)(2,1)}) %reduce-scatter.2.cloned.1.call-update) | async-done | bytes 2621456 | tf_op jit(solution)/shard_map/reduce_scatter | solution.py:68
  734.5 22.5 %convolution_convert_fusion = bf16[2,256,4096]{2,1,0:T(8,128)(2,1)} fusion(bf16[2,640,256]{2,1,0:T(8,128)(2,1)S(1)} %get-tuple-element.25, f32[2,640,4096]{2,0,1:T(2,128)} %bitcast.71, f32[2,640]{1,0:T(2,128)S(1)} %reshape.117), kind=kOutput, calls=%fused_computation.13 | convolution fusion | flops 2696937472 | bytes 25826304 | tf_op jit(solution)/shard_map/erf,erd->efd/dot_general | solution.py:52
  (62 shorter events, 83.7 us)
Async XLA Ops:
  7.2 40.4 %all-gather.5.cloned.1.call-start = ((), (), s32[]{:S(2)}) async-start(), calls=%async_computation.7 | async-start | bytes 1310720 | tf_op jit(solution)/shard_map/all_gather | solution.py:28
  37.7 41.5 %all-to-all-start = ((bf16[32,2,20]{2,1,0:T(2,128)(2,1)}), bf16[32,2,20]{2,1,0:T(2,128)(2,1)S(1)}, u32[]{:S(2)}, u32[]{:S(2)}) async-start(bf16[32,2,20]{2,1,0:T(2,128)(2,1)} %all_to_all.52), calls=%async_computation | async-start | bytes 32768 | tf_op jit(solution)/shard_map/all_to_all | solution.py:40
  79.1 182.1 %all-to-all-start.2 = ((bf16[64,20,4096]{2,1,0:T(8,128)(2,1)}), bf16[64,20,4096]{2,1,0:T(8,128)(2,1)}, u32[]{:S(2)}, u32[]{:S(2)}) async-start(bf16[64,20,4096]{2,1,0:T(8,128)(2,1)} %reshape.111), calls=%async_computation.2 | async-start | bytes 25165824 | tf_op jit(solution)/shard_map/all_to_all | solution.py:38
  86.6 26.6 %all-gather.3.cloned.1.call-start = ((), (), s32[]{:S(2)}) async-start(), calls=%async_computation.6 | async-start | bytes 1310720 | tf_op jit(solution)/shard_map/all_gather | solution.py:29
  261.2 204.3 %all-to-all-start.1 = ((bf16[64,20,4096]{2,1,0:T(8,128)(2,1)}), bf16[64,20,4096]{2,1,0:T(8,128)(2,1)}, u32[]{:S(2)}, u32[]{:S(2)}) async-start(bf16[64,20,4096]{2,1,0:T(8,128)(2,1)} %reshape.109), calls=%async_computation.1 | async-start | bytes 25165824 | tf_op jit(solution)/shard_map/all_to_all | solution.py:39
  290.9 415.0 %reduce-scatter.2.cloned.1.call-start = ((), (), s32[]{:S(2)}) async-start(), calls=%async_computation.8 | async-start | bytes 13107200 | tf_op jit(solution)/shard_map/reduce_scatter | solution.py:68
  518.8 10.5 %copy-start = (bf16[2,256,4096]{2,1,0:T(8,128)(2,1)S(1)}, bf16[2,256,4096]{2,1,0:T(8,128)(2,1)}, u32[]{:S(2)}) copy-start(bf16[2,256,4096]{2,1,0:T(8,128)(2,1)} %param.13) | copy-start | bytes 12582916
  560.6 11.0 %copy-start.1 = (bf16[2,640,256]{2,1,0:T(8,128)(2,1)}, bf16[2,640,256]{2,1,0:T(8,128)(2,1)S(1)}, u32[]{:S(2)}) copy-start(bf16[2,640,256]{2,1,0:T(8,128)(2,1)S(1)} %get-tuple-element.27) | copy-start | bytes 1966084
  615.3 96.5 %all-to-all-start.4 = ((bf16[2,32,20]{2,0,1:T(2,128)(2,1)}), bf16[2,32,20]{2,0,1:T(2,128)(2,1)S(1)}, u32[]{:S(2)}, u32[]{:S(2)}) async-start(bf16[2,32,20]{2,0,1:T(2,128)(2,1)} %copy.103), calls=%async_computation.5 | async-start | bytes 32768 | tf_op jit(solution)/shard_map/all_to_all | solution.py:76
  711.8 17.4 %slice-start = ((s8[10485760]{0:T(1024)(128)(4,1)}), s8[2097152]{0:T(1024)(128)(4,1)S(1)}, s32[]{:S(2)}) async-start(s8[10485760]{0:T(1024)(128)(4,1)} %bitcast.74), calls=%async_computation.9 | async-start | bytes 4194304
  711.8 52.8 %all-to-all-start.3 = ((bf16[2,32,20,1024]{3,0,2,1:T(2,128)(2,1)}), bf16[2,32,20,1024]{3,0,2,1:T(2,128)(2,1)}, u32[]{:S(2)}, u32[]{:S(2)}) async-start(bf16[2,32,20,1024]{3,0,2,1:T(2,128)(2,1)} %bitcast.76), calls=%async_computation.4 | async-start | bytes 5242880 | tf_op jit(solution)/shard_map/all_to_all | solution.py:75
  719.7 9.6 %slice-start.1 = ((s8[10485760]{0:T(1024)(128)(4,1)}), s8[4194304]{0:T(1024)(128)(4,1)S(1)}, s32[]{:S(2)}) async-start(s8[10485760]{0:T(1024)(128)(4,1)} %bitcast.74), calls=%async_computation.10 | async-start | bytes 8388608
  719.7 9.6 %slice-start.2 = ((s8[10485760]{0:T(1024)(128)(4,1)}), s8[4194304]{0:T(1024)(128)(4,1)S(1)}, s32[]{:S(2)}) async-start(s8[10485760]{0:T(1024)(128)(4,1)} %bitcast.74), calls=%async_computation.11 | async-start | bytes 8388608
  719.7 9.6 %copy-start.2 = (bf16[2,640,256]{2,1,0:T(8,128)(2,1)S(1)}, bf16[2,640,256]{2,1,0:T(8,128)(2,1)}, u32[]{:S(2)}) copy-start(bf16[2,640,256]{2,1,0:T(8,128)(2,1)} %copy-done.1) | copy-start | bytes 1966084
Sparse Core Ops, SparseCore 0:
  9.7 26.3 all-gather.4
  89.1 24.0 all-gather.2
  585.2 120.7 reduce-scatter.1
where the time goes:
time: 795 us; the launch traced here: 788 us
  waiting for transfers between devices  330 us (42%)
  local copies, waits for them, and re-layouts  187 us (24%)
  matrix products  124 us (16%)
  starting transfers between devices  87.8 us (11%)
  other arithmetic  36.3 us (5%)
  between operations  14.3 us (2%)
  blocking collectives  8.56 us (1%)
    all_to_all x1, waiting for transfers between devices, body(): lax.all_to_all(dy_send, 'dp', split_axis=0, concat_axis=1, tiled=True)  128 us
    all_to_all x1, waiting for transfers between devices, body(): lax.all_to_all(x_send, 'dp', split_axis=0, concat_axis=1, tiled=True)  117 us
    reduce_scatter x1, waiting for transfers between devices, body(): lax.psum_scatter(dx_part.astype(jnp.bfloat16), 'tensor', scatter_dimensio...  58.3 us
    all_to_all x2, local copies, waits for them, and re-layouts, body(): lax.all_to_all(x_send, 'dp', split_axis=0, concat_axis=1, tiled=True)  45.8 us
    scatter x3, local copies, waits for them, and re-layouts, place_rows(): jnp.zeros((total_rows,) + shape_rest, values.dtype).at[position].set(values)  42.9 us
    convert_element_type x2, local copies, waits for them, and re-layouts, body(): dy_rows.astype(jnp.float32)  39.6 us
    all_to_all x1, starting transfers between devices, body(): lax.all_to_all(route_send, 'dp', split_axis=1, concat_axis=0, tiled=True)  32.3 us
    all_to_all x1, starting transfers between devices, body(): lax.all_to_all(dy_send, 'dp', split_axis=0, concat_axis=1, tiled=True)  29.7 us
  transfers between devices with their start and end apart: 8, of which 4 were waited for; matrix products, arithmetic and copies ran while one was open for 27% of the time, Pallas kernels for 0%

commit v1 on v0

v1 whole, which is shorter than its diff:
```python
import functools

import jax
import jax.numpy as jnp
from jax import lax
from jax.experimental import pallas as pl
from jax.experimental.pallas import tpu as pltpu
from jax.sharding import PartitionSpec as P

BF = jnp.bfloat16
F32 = jnp.float32
BLK = 256
NT = (((1,), (1,)), ((), ()))
TN = (((0,), (0,)), ((), ()))
VMEM = 56 * 1024 * 1024


def params():
    return pltpu.CompilerParams(dimension_semantics=("arbitrary",), vmem_limit_bytes=VMEM)


def first_expert(rows, cap):
    return lax.broadcasted_iota(jnp.int32, (rows, 1), 0) % (2 * cap) < cap


def fwd_kernel(per, nq, cap, xq, xp, wg, wu, act, c1, c2, a1, a2):
    i = pl.program_id(0)
    rows = a1.shape[0]

    @pl.when(i == 0)
    def _():
        a1[...] = jnp.zeros_like(a1)
        a2[...] = jnp.zeros_like(a2)

    def add(x):
        for e in range(2):
            at = pl.ds(e * BLK, BLK)
            a1[:, at] += jnp.dot(x, wg[e], preferred_element_type=F32)
            a2[:, at] += jnp.dot(x, wu[e], preferred_element_type=F32)

    @pl.when(i % per < nq)
    def _():
        add(xq[0])

    @pl.when(i % per >= nq)
    def _():
        add(xp[...])

    @pl.when(i == pl.num_programs(0) - 1)
    def _():
        mask = first_expert(rows, cap)
        h1 = jnp.where(mask, a1[:, :BLK], a1[:, BLK:])
        h2 = jnp.where(mask, a2[:, :BLK], a2[:, BLK:])
        s = jax.nn.sigmoid(h1)
        hs = h1 * s
        act[...] = (hs * h2).astype(BF)
        c2[...] = hs
        c1[...] = h2 * s * (1.0 + h1 * (1.0 - s))


def bwd_kernel(per, nq, cap, dq, dp, wd, act, c1, c2, d1, d2, q, acc):
    i = pl.program_id(0)
    rows = acc.shape[0]

    @pl.when(i == 0)
    def _():
        acc[...] = jnp.zeros_like(acc)

    def add(x):
        for e in range(2):
            at = pl.ds(e * BLK, BLK)
            acc[:, at] += lax.dot_general(x, wd[e], NT, preferred_element_type=F32)

    @pl.when(i % per < nq)
    def _():
        add(dq[0])

    @pl.when(i % per >= nq)
    def _():
        add(dp[...])

    @pl.when(i == pl.num_programs(0) - 1)
    def _():
        da = jnp.where(first_expert(rows, cap), acc[:, :BLK], acc[:, BLK:])
        d1[...] = (da * c1[...]).astype(BF)
        d2[...] = (da * c2[...]).astype(BF)
        q[...] = jnp.sum(da * act[...].astype(F32), axis=1, keepdims=True)


def dx_kernel(per, nq, cap, d1, d2, wg, wu, oq, op):
    i = pl.program_id(0)
    mask = first_expert(d1.shape[0], cap)
    zero = jnp.zeros((), BF)

    def part():
        total = None
        for d, w in ((d1, wg), (d2, wu)):
            for e in range(2):
                lhs = jnp.where(mask, d[...], zero) if e == 0 else jnp.where(mask, zero, d[...])
                term = lax.dot_general(lhs, w[e], NT, preferred_element_type=F32)
                total = term if total is None else total + term
        return total.astype(BF)

    @pl.when(i % per < nq)
    def _():
        oq[0] = part()

    @pl.when(i % per >= nq)
    def _():
        op[...] = part()


def grad_kernel(per, nq, cap, xq, xp, dq, dp, d1, d2, act, gg, gu, gd, right, left):
    i = pl.program_id(0)

    @pl.when(i == 0)
    def _():
        mask = first_expert(d1.shape[0], cap)
        zero = jnp.zeros((), BF)
        for at, v in ((0, d1), (2, d2)):
            right[:, at * BLK:(at + 1) * BLK] = jnp.where(mask, v[...], zero)
            right[:, (at + 1) * BLK:(at + 2) * BLK] = jnp.where(mask, zero, v[...])
        left[:BLK] = jnp.where(mask, act[...], zero).T
        left[BLK:] = jnp.where(mask, zero, act[...]).T

    def run(x, d):
        out = lax.dot_general(x, right[...], TN, preferred_element_type=F32).astype(BF)
        gg[0] = out[:, :BLK]
        gg[1] = out[:, BLK:2 * BLK]
        gu[0] = out[:, 2 * BLK:3 * BLK]
        gu[1] = out[:, 3 * BLK:]
        down = jnp.dot(left[...], d, preferred_element_type=F32).astype(BF)
        gd[0] = down[:BLK]
        gd[1] = down[BLK:]

    @pl.when(i % per < nq)
    def _():
        run(xq[0], dq[0])

    @pl.when(i % per >= nq)
    def _():
        run(xp[...], dp[...])


def body(tokens, cotangent, expert_ids, gates, w_gate, w_up, w_down):
    tok, share = tokens.shape
    top = expert_ids.shape[1]
    local, width, ff = w_gate.shape
    n_dp = lax.axis_size("dp")
    n_t = lax.axis_size("tensor")
    experts = local * n_dp
    cap = max(2, tok * top * 5 // (4 * experts))
    rows = experts * cap
    per_dev = local * cap
    per = share // BLK
    nq = per - 1
    qw = nq * BLK
    steps = width // BLK

    eye_e = jnp.arange(experts, dtype=jnp.int32)
    hot = expert_ids[:, :, None] == eye_e[None, None, :]
    names = jnp.sum(hot.astype(F32), axis=1)
    gate_of = jnp.sum(jnp.where(hot, gates.astype(F32)[:, :, None], 0.0), axis=1)
    tri = (jnp.arange(tok)[:, None] > jnp.arange(tok)[None, :]).astype(BF)
    slot = jnp.dot(tri, names.astype(BF), preferred_element_type=F32)
    slot = jnp.where(names > 0, slot, -1.0)
    row_id = jnp.arange(rows, dtype=jnp.int32)
    spread = (row_id[:, None] // cap == eye_e[None, :]).astype(BF)
    slot_rows = lax.dot_general(spread, slot.astype(BF), NT, preferred_element_type=F32)
    gate_rows = lax.dot_general(spread, gate_of.astype(BF), NT, preferred_element_type=F32)
    placed = slot_rows == (row_id % cap).astype(F32)[:, None]
    place = placed.astype(BF)
    place_g = jnp.where(placed, gate_rows, 0.0).astype(BF)

    def to_experts(v):
        v = v.reshape(n_dp, per_dev, v.shape[1])
        return lax.all_to_all(v, "dp", 0, 0, tiled=True).reshape(rows, v.shape[2])

    def rows_of(matrix, v):
        return jnp.dot(matrix, v, preferred_element_type=F32).astype(BF)

    tail = jnp.stack([tokens[:, qw:], cotangent[:, qw:]])
    tail = lax.all_gather(tail, "tensor", axis=2, tiled=True)
    xq = to_experts(rows_of(place, tokens[:, :qw]))
    xq = lax.all_gather(xq, "tensor", axis=0)
    dq = to_experts(rows_of(place_g, cotangent[:, :qw]))
    dq = lax.all_gather(dq, "tensor", axis=0)
    xp = to_experts(rows_of(place, tail[0]))
    dp = to_experts(rows_of(place_g, tail[1]))

    q_spec = pl.BlockSpec((1, rows, BLK), lambda i: (i // per, 0, jnp.minimum(i % per, nq - 1)))
    p_spec = pl.BlockSpec((rows, BLK), lambda i: (0, i // per))
    w_spec = pl.BlockSpec((local, BLK, ff), lambda i: (0, i, 0))
    wd_spec = pl.BlockSpec((local, ff, BLK), lambda i: (0, 0, i))
    whole = pl.BlockSpec((rows, ff), lambda i: (0, 0))
    flops = 2 * 2 * rows * width * ff
    row_bytes = rows * width * 2
    w_bytes = local * width * ff * 2

    act, c1, c2 = pl.pallas_call(
        functools.partial(fwd_kernel, per, nq, cap),
        grid=(steps,),
        in_specs=[q_spec, p_spec, w_spec, w_spec],
        out_specs=[whole, whole, whole],
        out_shape=[
            jax.ShapeDtypeStruct((rows, ff), BF),
            jax.ShapeDtypeStruct((rows, ff), F32),
            jax.ShapeDtypeStruct((rows, ff), F32),
        ],
        scratch_shapes=[pltpu.VMEM((rows, 2 * ff), F32), pltpu.VMEM((rows, 2 * ff), F32)],
        compiler_params=params(),
        cost_estimate=pl.CostEstimate(
            flops=2 * flops, bytes_accessed=row_bytes + 2 * w_bytes, transcendentals=0
        ),
        name="hidden",
    )(xq, xp, w_gate, w_up)

    d1, d2, q = pl.pallas_call(
        functools.partial(bwd_kernel, per, nq, cap),
        grid=(steps,),
        in_specs=[q_spec, p_spec, wd_spec, whole, whole, whole],
        out_specs=[whole, whole, pl.BlockSpec((rows, 1), lambda i: (0, 0))],
        out_shape=[
            jax.ShapeDtypeStruct((rows, ff), BF),
            jax.ShapeDtypeStruct((rows, ff), BF),
            jax.ShapeDtypeStruct((rows, 1), F32),
        ],
        scratch_shapes=[pltpu.VMEM((rows, 2 * ff), F32)],
        compiler_params=params(),
        cost_estimate=pl.CostEstimate(
            flops=flops, bytes_accessed=row_bytes + w_bytes, transcendentals=0
        ),
        name="hidden_grad",
    )(dq, dp, w_down, act, c1, c2)

    oq, op = pl.pallas_call(
        functools.partial(dx_kernel, per, nq, cap),
        grid=(steps,),
        in_specs=[whole, whole, w_spec, w_spec],
        out_specs=[q_spec, p_spec],
        out_shape=[
            jax.ShapeDtypeStruct((n_t, rows, qw), BF),
            jax.ShapeDtypeStruct((rows, n_t * (share - qw)), BF),
        ],
        compiler_params=params(),
        cost_estimate=pl.CostEstimate(
            flops=2 * flops, bytes_accessed=row_bytes + 2 * w_bytes, transcendentals=0
        ),
        name="row_grad",
    )(d1, d2, w_gate, w_up)

    grad_gate, grad_up, grad_down = pl.pallas_call(
        functools.partial(grad_kernel, per, nq, cap),
        grid=(steps,),
        in_specs=[q_spec, p_spec, q_spec, p_spec, whole, whole, whole],
        out_specs=[w_spec, w_spec, wd_spec],
        out_shape=[
            jax.ShapeDtypeStruct(w_gate.shape, BF),
            jax.ShapeDtypeStruct(w_up.shape, BF),
            jax.ShapeDtypeStruct(w_down.shape, BF),
        ],
        scratch_shapes=[pltpu.VMEM((rows, 4 * ff), BF), pltpu.VMEM((2 * ff, rows), BF)],
        compiler_params=params(),
        cost_estimate=pl.CostEstimate(
            flops=3 * flops, bytes_accessed=2 * row_bytes + 3 * w_bytes, transcendentals=0
        ),
        name="weight_grads",
    )(xq, xp, dq, dp, d1, d2, act)

    back_q = to_experts(lax.psum_scatter(oq, "tensor", scatter_dimension=0))
    back_p = to_experts(op)
    q_back = lax.all_to_all(q.reshape(n_dp, per_dev), "dp", 0, 0, tiled=True).reshape(rows, 1)

    tok_q = lax.dot_general(place, back_q, TN, preferred_element_type=F32).astype(BF)
    tok_p = lax.dot_general(place, back_p, TN, preferred_element_type=F32)
    tok_p = lax.psum_scatter(tok_p, "tensor", scatter_dimension=1, tiled=True).astype(BF)
    grad_tokens = jnp.concatenate([tok_q, tok_p], axis=1)

    q_of = lax.dot_general(
        place, (spread.astype(F32) * q_back).astype(BF), TN, preferred_element_type=F32
    )
    q_of = jnp.sum(jnp.where(hot, q_of[:, None, :], 0.0), axis=2)
    grad_gates = (lax.psum(q_of, "tensor") / gates.astype(F32)).astype(BF)
    return grad_tokens, grad_gates, grad_gate, grad_up, grad_down


def solution(mesh):
    in_specs = (
        P("dp", "tensor"),
        P("dp", "tensor"),
        P("dp", None),
        P("dp", None),
        P("dp", None, "tensor"),
        P("dp", None, "tensor"),
        P("dp", "tensor", None),
    )
    out_specs = (
        P("dp", "tensor"),
        P("dp", None),
        P("dp", None, "tensor"),
        P("dp", None, "tensor"),
        P("dp", "tensor", None),
    )
    return jax.shard_map(body, mesh=mesh, in_specs=in_specs, out_specs=out_specs, check_vma=False)
```

time: 795 us -> 384 us (0.48)
  waiting for transfers between devices: 330 us -> 138 us
  local copies, waits for them, and re-layouts: 187 us -> 3.64 us
  matrix products: 124 us -> 11.3 us
  Pallas kernels: 0 us -> 90.5 us
  blocking collectives: 8.56 us -> 88.2 us
  starting transfers between devices: 87.8 us -> 30.9 us
  other arithmetic: 36.3 us -> 4.64 us
    all_to_all x5, waiting for transfers between devices: 245 us -> 80.9 us  [the longest x4 75.4 us: to_experts(): return lax.all_to_all(v, 'dp', 0, 0, tiled=True).reshape(rows, v.shape[2])]
    dot_general x9, matrix products: 124 us -> 11.3 us  [the longest x4 7.87 us: rows_of(): return jnp.dot(matrix, v, preferred_element_type=F32).astype(BF)]
    pallas_call x0 -> x4, Pallas kernels: none -> 90.5 us  [the longest x1 27.6 us: body(): pl.pallas_call(functools.partial(grad_kernel, per, nq, cap), grid=(steps,...]
    all_to_all x0 -> x2, blocking collectives: none -> 67 us  [to_experts(): return lax.all_to_all(v, 'dp', 0, 0, tiled=True).reshape(rows, v.shape[2])]
    all_to_all x5, starting transfers between devices: 87.1 us -> 30.6 us  [the longest x4 26.1 us: to_experts(): return lax.all_to_all(v, 'dp', 0, 0, tiled=True).reshape(rows, v.shape[2])]
    all_to_all x4 -> x2, local copies, waits for them, and re-layouts: 50.9 us -> 1.21 us  [body(): lax.all_to_all(q.reshape(n_dp, per_dev), 'dp', 0, 0, tiled=True)]
    scatter x3 -> x0, local copies, waits for them, and re-layouts: 42.9 us -> none  [place_rows(): jnp.zeros((total_rows,) + shape_rest, values.dtype).at[position].set(values)]
    convert_element_type x4 -> x0, local copies, waits for them, and re-layouts: 39.7 us -> none  [the longest x2 39.6 us: body(): dy_rows.astype(jnp.float32)]
  transfers between devices with their start and end apart: 8 -> 9, of which waited for: 4 -> 6; matrix products, arithmetic and copies ran while one was open for 27% -> 3% of each run, Pallas kernels for 0% -> 13%
where the time goes in v1:
time: 384 us; the launch traced here: 381 us
  waiting for transfers between devices  138 us (36%)
  Pallas kernels  90.5 us (24%)
  blocking collectives  88.2 us (23%)
  starting transfers between devices  30.9 us (8%)
  between operations  14 us (4%)
  matrix products  11.3 us (3%)
  other arithmetic  4.64 us (1%)
    all_to_all x4, waiting for transfers between devices, to_experts(): return lax.all_to_all(v, 'dp', 0, 0, tiled=True).reshape(rows, v.shape[2])  75.4 us
    all_to_all x2, blocking collectives, to_experts(): return lax.all_to_all(v, 'dp', 0, 0, tiled=True).reshape(rows, v.shape[2])  67 us
    all_gather x1, waiting for transfers between devices, body(): dq = lax.all_gather(dq, 'tensor', axis=0)  32.6 us
    pallas_call x1, Pallas kernels, body(): pl.pallas_call(functools.partial(grad_kernel, per, nq, cap), grid=(steps,...  27.6 us
    all_to_all x4, starting transfers between devices, to_experts(): return lax.all_to_all(v, 'dp', 0, 0, tiled=True).reshape(rows, v.shape[2])  26.1 us
    reduce_scatter x1, waiting for transfers between devices, body(): back_q = to_experts(lax.psum_scatter(oq, 'tensor', scatter_dimension=0))  24.6 us
    pallas_call x1, Pallas kernels, body(): pl.pallas_call(functools.partial(dx_kernel, per, nq, cap), grid=(steps,),...  22.5 us
    pallas_call x1, Pallas kernels, body(): pl.pallas_call(functools.partial(fwd_kernel, per, nq, cap), grid=(steps,)...  22 us
  transfers between devices with their start and end apart: 9, of which 6 were waited for; matrix products, arithmetic and copies ran while one was open for 3% of the time, Pallas kernels for 13%

profile of v1, /device:TPU:1, one launch (start us, length us, event | category | flops | bytes accessed | tf_op | source)
XLA Modules:
  0.0 381.3 jit_solution(2869943137834251632)
XLA Ops:
  9.1 1.6 convolution_convert_fusion.2
  10.7 36.3 %all_to_all.39 = bf16[32,40,768]{2,1,0:T(8,128)(2,1)} all-to-all(bf16[32,40,768]{2,1,0:T(8,128)(2,1)S(1)} %bitcast.37), channel_id=1, replica_groups=mesh['dp'=32,'tensor'=4] {'dp'}, dimensions={0} | all-to-all | bytes 3932160 | tf_op jit(solution)/shard_map/all_to_all | solution.py:177
  48.2 30.6 %all_to_all.40 = bf16[32,40,768]{2,1,0:T(8,128)(2,1)} all-to-all(bf16[32,40,768]{2,1,0:T(8,128)(2,1)S(1)} %bitcast.38), channel_id=1, replica_groups=mesh['dp'=32,'tensor'=4] {'dp'}, dimensions={0} | all-to-all | bytes 3932160 | tf_op jit(solution)/shard_map/all_to_all | solution.py:177
  79.7 14.5 %all_gather.10 = bf16[2,128,1024]{2,1,0:T(8,128)(2,1)S(1)} all-gather(bf16[2,128,256]{2,1,0:T(8,128)(2,1)S(1)} %pad_maximum_fusion.1), channel_id=1, replica_groups=mesh['dp'=32,'tensor'=4] {'tensor'}, dimensions={2}, use_global_device_ids=true | all-gather | bytes 655360 | tf_op jit(solution)/shard_map/all_gather | solution.py:183
  94.2 2.3 convolution_convert_fusion
  96.5 5.1 %all-to-all-start.3 = ((bf16[32,40,1024]{2,1,0:T(8,128)(2,1)}), bf16[32,40,1024]{2,1,0:T(8,128)(2,1)S(1)}, u32[]{:S(2)}, u32[]{:S(2)}) async-start(bf16[32,40,1024]{2,1,0:T(8,128)(2,1)} %bitcast.10), calls=%async_computation.3 | async-start | bytes 5242880 | tf_op jit(solution)/shard_map/all_to_all | solution.py:177
  101.6 3.3 convolution_convert_fusion.1
  104.9 30.7 %all-to-all-done.3 = bf16[32,40,1024]{2,1,0:T(8,128)(2,1)S(1)} async-done(((bf16[32,40,1024]{2,1,0:T(8,128)(2,1)}), bf16[32,40,1024]{2,1,0:T(8,128)(2,1)S(1)}, u32[]{:S(2)}, u32[]{:S(2)}) %all-to-all-start.3) | async-done | bytes 2621472 | tf_op jit(solution)/shard_map/all_to_all | solution.py:177
  135.6 1.5 copy-done
  137.1 5.4 %all-to-all-start.1 = ((bf16[32,40,1024]{2,1,0:T(8,128)(2,1)}), bf16[32,40,1024]{2,1,0:T(8,128)(2,1)}, u32[]{:S(2)}, u32[]{:S(2)}) async-start(bf16[32,40,1024]{2,1,0:T(8,128)(2,1)} %bitcast.5), calls=%async_computation.1 | async-start | bytes 5242880 | tf_op jit(solution)/shard_map/all_to_all | solution.py:177
  142.7 22.0 %hidden.1 = (bf16[1280,256]{1,0:T(8,128)(2,1)}, f32[1280,256]{1,0:T(8,128)}, f32[1280,256]{1,0:T(8,128)}) custom-call(bf16[4,1280,768]{2,1,0:T(8,128)(2,1)} %all-gather.5.cloned.1.call-done.xq, bf16[1280,1024]{1,0:T(8,128)(2,1)} %bitcast.39, bf16[2,4096,256]{2,1,0:T(8,128)(2,1)} %wg.3, bf16[2,4096,256]{2,1,0:T(8,128)(2,1)} %wu.3), custom_call_target="tpu_custom_call" | custom-call | flops 10737418240 | bytes 18874368 | tf_op jit(solution)/shard_map/hidden/pallas_call | solution.py:200
  164.7 11.8 %all-to-all-done.1 = bf16[32,40,1024]{2,1,0:T(8,128)(2,1)} async-done(((bf16[32,40,1024]{2,1,0:T(8,128)(2,1)}), bf16[32,40,1024]{2,1,0:T(8,128)(2,1)}, u32[]{:S(2)}, u32[]{:S(2)}) %all-to-all-start.1) | async-done | bytes 2621472 | tf_op jit(solution)/shard_map/all_to_all | solution.py:177
  176.5 32.6 %all-gather.3.cloned.1.call-done.dq = bf16[4,1280,768]{2,1,0:T(8,128)(2,1)} async-done(((bf16[1,1280,768]{2,1,0:T(8,128)(2,1)}), bf16[4,1280,768]{2,1,0:T(8,128)(2,1)}) %all-gather.3.cloned.1.call-update) | async-done | bytes 7864336 | tf_op jit(solution)/shard_map/all_gather | solution.py:187
  209.1 18.4 %hidden_grad.1 = (bf16[1280,256]{1,0:T(8,128)(2,1)}, bf16[1280,256]{1,0:T(8,128)(2,1)}, f32[1280,1]{1,0:T(8,128)}) custom-call(bf16[4,1280,768]{2,1,0:T(8,128)(2,1)} %all-gather.3.cloned.1.call-done.dq, bf16[1280,1024]{1,0:T(8,128)(2,1)} %bitcast.6.dp, bf16[2,256,4096]{2,1,0:T(8,128)(2,1)} %wd.1, bf16[1280,256]{1,0:T(8,128)(2,1)} %get-tuple-element.16.act, ...), custom_call_target="tpu_custom_call" | custom-call | flops 5368709120 | bytes 14680064 | tf_op jit(solution)/shard_map/hidden_grad/pallas_call | solution.py:218
  227.5 22.5 %row_grad.1 = (bf16[4,1280,768]{2,1,0:T(8,128)(2,1)}, bf16[1280,1024]{1,0:T(8,128)(2,1)}) custom-call(bf16[1280,256]{1,0:T(8,128)(2,1)} %get-tuple-element.19.d1, bf16[1280,256]{1,0:T(8,128)(2,1)} %get-tuple-element.20.d2, bf16[2,4096,256]{2,1,0:T(8,128)(2,1)} %wg.3, bf16[2,4096,256]{2,1,0:T(8,128)(2,1)} %wu.3), custom_call_target="tpu_custom_call" | custom-call | flops 10737418240 | bytes 18874368 | tf_op jit(solution)/shard_map/row_grad/pallas_call | solution.py:236
  250.0 7.9 %all-to-all-start.5 = ((bf16[32,40,1024]{2,1,0:T(8,128)(2,1)}), bf16[32,40,1024]{2,1,0:T(8,128)(2,1)S(1)}, u32[]{:S(2)}, u32[]{:S(2)}) async-start(bf16[32,40,1024]{2,1,0:T(8,128)(2,1)} %bitcast.41), calls=%async_computation.6 | async-start | bytes 5242880 | tf_op jit(solution)/shard_map/all_to_all | solution.py:177
  258.8 32.9 %all-to-all-done.5 = bf16[32,40,1024]{2,1,0:T(8,128)(2,1)S(1)} async-done(((bf16[32,40,1024]{2,1,0:T(8,128)(2,1)}), bf16[32,40,1024]{2,1,0:T(8,128)(2,1)S(1)}, u32[]{:S(2)}, u32[]{:S(2)}) %all-to-all-start.5) | async-done | bytes 2621472 | tf_op jit(solution)/shard_map/all_to_all | solution.py:177
  291.8 4.5 %all-to-all-start.6 = ((f32[32,1,40]{2,1,0:T(1,128)}), f32[32,1,40]{2,1,0:T(1,128)S(1)}, u32[]{:S(2)}, u32[]{:S(2)}) async-start(f32[32,1,40]{2,1,0:T(1,128)} %bitcast.16), calls=%async_computation.8 | async-start | bytes 32768 | tf_op jit(solution)/shard_map/all_to_all | solution.py:272
  296.3 1.4 fusion.26
  297.7 5.5 %all-to-all-done.6 = f32[32,1,40]{2,1,0:T(1,128)S(1)} async-done(((f32[32,1,40]{2,1,0:T(1,128)}), f32[32,1,40]{2,1,0:T(1,128)S(1)}, u32[]{:S(2)}, u32[]{:S(2)}) %all-to-all-start.6) | async-done | bytes 5152 | tf_op jit(solution)/shard_map/all_to_all | solution.py:272
  303.2 24.6 %reduce-scatter.3.cloned.1.call-done = bf16[1,1280,768]{2,1,0:T(8,128)(2,1)} async-done(((bf16[4,1280,768]{2,1,0:T(8,128)(2,1)}), bf16[1,1280,768]{2,1,0:T(8,128)(2,1)}) %reduce-scatter.3.cloned.1.call-update) | async-done | bytes 1966096 | tf_op jit(solution)/shard_map/reduce_scatter | solution.py:270
  327.9 7.7 %all-to-all-start.4 = ((bf16[32,40,768]{2,1,0:T(8,128)(2,1)}), bf16[32,40,768]{2,1,0:T(8,128)(2,1)S(1)}, u32[]{:S(2)}, u32[]{:S(2)}) async-start(bf16[32,40,768]{2,1,0:T(8,128)(2,1)} %bitcast.42), calls=%async_computation.5 | async-start | bytes 3932160 | tf_op jit(solution)/shard_map/all_to_all | solution.py:177
  335.6 27.6 %weight_grads.1 = (bf16[2,4096,256]{2,1,0:T(8,128)(2,1)}, bf16[2,4096,256]{2,1,0:T(8,128)(2,1)}, bf16[2,256,4096]{2,1,0:T(8,128)(2,1)}) custom-call(bf16[4,1280,768]{2,1,0:T(8,128)(2,1)} %all-gather.5.cloned.1.call-done.xq, bf16[1280,1024]{1,0:T(8,128)(2,1)} %bitcast.40, bf16[4,1280,768]{2,1,0:T(8,128)(2,1)} %all-gather.3.cloned.1.call-done.dq, ...), custom_call_target="tpu_custom_call" | custom-call | flops 16106127360 | bytes 33554432 | tf_op jit(solution)/shard_map/weight_grads/pallas_call | solution.py:252
  365.3 6.7 %psum.7 = f32[128,8]{0,1:T(8,128)S(1)} all-reduce(f32[128,8]{0,1:T(8,128)S(1)} %select_reduce_fusion), channel_id=1, replica_groups=mesh['dp'=32,'tensor'=4] {'tensor'}, use_global_device_ids=true, to_apply=%region_5.6 | all-reduce | flops 1024 | bytes 8192 | tf_op jit(solution)/shard_map/psum | solution.py:283
  (42 shorter events, 9.9 us)
Async XLA Ops:
  7.2 135.6 %all-gather.5.cloned.1.call-start = ((), (), s32[]{:S(2)}) async-start(), calls=%async_computation.10 | async-start | bytes 9830400 | tf_op jit(solution)/shard_map/all_gather | solution.py:185
  10.7 36.8 %copy-start.3 = (bf16[128,1024]{1,0:T(8,128)(2,1)S(1)}, bf16[128,1024]{1,0:T(8,128)(2,1)}, u32[]{:S(2)}) copy-start(bf16[128,1024]{1,0:T(8,128)(2,1)} %param.8) | copy-start | bytes 786436
  47.1 162.0 %all-gather.3.cloned.1.call-start = ((), (), s32[]{:S(2)}) async-start(), calls=%async_computation.9 | async-start | bytes 9830400 | tf_op jit(solution)/shard_map/all_gather | solution.py:187
  47.5 31.3 %copy-start.1 = (bf16[1280,128]{1,0:T(8,128)(2,1)}, bf16[1280,128]{1,0:T(8,128)(2,1)S(1)}, u32[]{:S(2)}) copy-start(bf16[1280,128]{1,0:T(8,128)(2,1)S(1)} %fusion) | copy-start | bytes 983044
  96.5 39.1 %all-to-all-start.3 = ((bf16[32,40,1024]{2,1,0:T(8,128)(2,1)}), bf16[32,40,1024]{2,1,0:T(8,128)(2,1)S(1)}, u32[]{:S(2)}, u32[]{:S(2)}) async-start(bf16[32,40,1024]{2,1,0:T(8,128)(2,1)} %bitcast.10), calls=%async_computation.3 | async-start | bytes 5242880 | tf_op jit(solution)/shard_map/all_to_all | solution.py:177
  135.6 1.5 copy-start
  137.1 39.5 %all-to-all-start.1 = ((bf16[32,40,1024]{2,1,0:T(8,128)(2,1)}), bf16[32,40,1024]{2,1,0:T(8,128)(2,1)}, u32[]{:S(2)}, u32[]{:S(2)}) async-start(bf16[32,40,1024]{2,1,0:T(8,128)(2,1)} %bitcast.5), calls=%async_computation.1 | async-start | bytes 5242880 | tf_op jit(solution)/shard_map/all_to_all | solution.py:177
  142.5 185.4 %reduce-scatter.3.cloned.1.call-start = ((), (), s32[]{:S(2)}) async-start(), calls=%async_computation.11 | async-start | bytes 9830400 | tf_op jit(solution)/shard_map/reduce_scatter | solution.py:270
  250.0 7.9 %copy-start.2 = (f32[1280,1]{1,0:T(8,128)S(1)}, f32[1280,1]{1,0:T(8,128)}, u32[]{:S(2)}) copy-start(f32[1280,1]{1,0:T(8,128)} %get-tuple-element.23) | copy-start | bytes 15364
  250.0 41.8 %all-to-all-start.5 = ((bf16[32,40,1024]{2,1,0:T(8,128)(2,1)}), bf16[32,40,1024]{2,1,0:T(8,128)(2,1)S(1)}, u32[]{:S(2)}, u32[]{:S(2)}) async-start(bf16[32,40,1024]{2,1,0:T(8,128)(2,1)} %bitcast.41), calls=%async_computation.6 | async-start | bytes 5242880 | tf_op jit(solution)/shard_map/all_to_all | solution.py:177
  291.8 11.4 %all-to-all-start.6 = ((f32[32,1,40]{2,1,0:T(1,128)}), f32[32,1,40]{2,1,0:T(1,128)S(1)}, u32[]{:S(2)}, u32[]{:S(2)}) async-start(f32[32,1,40]{2,1,0:T(1,128)} %bitcast.16), calls=%async_computation.8 | async-start | bytes 32768 | tf_op jit(solution)/shard_map/all_to_all | solution.py:272
  296.2 76.3 %reduce-scatter.5.cloned.1.call-start = ((), (), s32[]{:S(2)}) async-start(), calls=%async_computation.12 | async-start | bytes 655360 | tf_op jit(solution)/shard_map/reduce_scatter | solution.py:276
  327.9 45.6 %all-to-all-start.4 = ((bf16[32,40,768]{2,1,0:T(8,128)(2,1)}), bf16[32,40,768]{2,1,0:T(8,128)(2,1)S(1)}, u32[]{:S(2)}, u32[]{:S(2)}) async-start(bf16[32,40,768]{2,1,0:T(8,128)(2,1)} %bitcast.42), calls=%async_computation.5 | async-start | bytes 3932160 | tf_op jit(solution)/shard_map/all_to_all | solution.py:177
  335.6 29.6 %copy-start.4 = (s32[128,8]{0,1:T(8,128)S(1)}, s32[128,8]{0,1:T(8,128)}, u32[]{:S(2)}) copy-start(s32[128,8]{0,1:T(8,128)} %param.9) | copy-start | bytes 12292
  335.6 36.4 %copy-start.5 = (bf16[128,8]{0,1:T(8,128)(2,1)S(1)}, bf16[128,8]{0,1:T(8,128)(2,1)}, u32[]{:S(2)}) copy-start(bf16[128,8]{0,1:T(8,128)(2,1)} %param.10) | copy-start | bytes 6148
Sparse Core Ops, SparseCore 0:
  47.2 80.4 all-gather.4
  129.4 79.6 all-gather.2
  250.1 77.7 reduce-scatter.2
  330.1 19.5 reduce-scatter.4

commit v2 on v0

v2 whole, which is shorter than its diff:
```python
import functools

import jax
import jax.numpy as jnp
from jax import lax
from jax.experimental import pallas as pl
from jax.experimental.pallas import tpu as pltpu
from jax.sharding import PartitionSpec as P

BF = jnp.bfloat16
F32 = jnp.float32
BLK = 256
NT = (((1,), (1,)), ((), ()))
TN = (((0,), (0,)), ((), ()))
VMEM = 56 * 1024 * 1024
WHOLE = pl.BlockSpec(memory_space=pltpu.VMEM)
SMEM = pl.BlockSpec(memory_space=pltpu.SMEM)


def params():
    return pltpu.CompilerParams(dimension_semantics=("arbitrary",), vmem_limit_bytes=VMEM)


def cost(flops, nbytes):
    return pl.CostEstimate(flops=flops, bytes_accessed=nbytes, transcendentals=0)


def first_expert(start, rows, cap):
    return (start + lax.broadcasted_iota(jnp.int32, (rows, 1), 0)) % (2 * cap) < cap


def pieces(places, share, n_t, at, refs):
    for place, ref in zip(places, refs):
        column = 0
        for s, device, first, width in place:
            if s is not None:
                device = (at[0] + s) % n_t
            begin = pl.multiple_of(device * share + first, BLK)
            yield ref[:, column:column + width], begin, width
            column += width


def fwd_kernel(places, share, cap, at, *refs):
    xs, (wg, wu, act, act_t, c1, c2) = refs[:-6], refs[-6:]
    rows = act.shape[0]
    sums = [None] * 4
    for x, begin, width in pieces(places, share, wg.shape[1] // share, at, xs):
        for k, (w, e) in enumerate(((wg, 0), (wg, 1), (wu, 0), (wu, 1))):
            term = jnp.dot(x, w[e, pl.ds(begin, width), :], preferred_element_type=F32)
            sums[k] = term if sums[k] is None else sums[k] + term
    mask = first_expert(pl.program_id(0) * rows, rows, cap)
    h1 = jnp.where(mask, sums[0], sums[1])
    h2 = jnp.where(mask, sums[2], sums[3])
    s = jax.nn.sigmoid(h1)
    hs = h1 * s
    a = hs * h2
    act[...] = a.astype(BF)
    act_t[:BLK] = jnp.where(mask, a, 0.0).T.astype(BF)
    act_t[BLK:] = jnp.where(mask, 0.0, a).T.astype(BF)
    c2[...] = hs
    c1[...] = h2 * s * (1.0 + h1 * (1.0 - s))


def bwd_kernel(places, share, cap, at, *refs):
    ds, (wd, act, c1, c2, dh, q) = refs[:-6], refs[-6:]
    rows = ds[0].shape[0]
    sums = [None] * 2
    for d, begin, width in pieces(places, share, wd.shape[2] // share, at, ds):
        for e in range(2):
            w = wd[e, :, pl.ds(begin, width)]
            term = lax.dot_general(d, w, NT, preferred_element_type=F32)
            sums[e] = term if sums[e] is None else sums[e] + term
    mask = first_expert(pl.program_id(0) * rows, rows, cap)
    da = jnp.where(mask, sums[0], sums[1])
    d1 = da * c1[...]
    d2 = da * c2[...]
    for k, v in enumerate((d1, d2)):
        dh[:, 2 * k * BLK:(2 * k + 1) * BLK] = jnp.where(mask, v, 0.0).astype(BF)
        dh[:, (2 * k + 1) * BLK:(2 * k + 2) * BLK] = jnp.where(mask, 0.0, v).astype(BF)
    q[...] = jnp.sum(da * act[...].astype(F32), axis=1, keepdims=True)


def dx_kernel(at, dh, wg, wu, out):
    w = jnp.concatenate([wg[0], wg[1], wu[0], wu[1]], axis=1)
    out[...] = lax.dot_general(dh[...], w, NT, preferred_element_type=F32).astype(BF)


def grad_kernel(nx, nq, at, xq, xp, dq, dp, dh, act_t, *refs):
    gg, gu, gd = refs[-3:]
    i = pl.program_id(0)

    def run(x, d):
        out = lax.dot_general(x[...], dh[...], TN, preferred_element_type=F32).astype(BF)
        gg[0] = out[:, :BLK]
        gg[1] = out[:, BLK:2 * BLK]
        gu[0] = out[:, 2 * BLK:3 * BLK]
        gu[1] = out[:, 3 * BLK:]
        down = jnp.dot(act_t[...], d[...], preferred_element_type=F32).astype(BF)
        gd[0] = down[:BLK]
        gd[1] = down[BLK:]

    @pl.when(i < nx)
    def _():
        run(xq, dq)

    @pl.when((i >= nx) & (i < nq))
    def _():
        run(xp, dq)

    @pl.when(i >= nq)
    def _():
        run(xp, dp)


def body(tokens, cotangent, expert_ids, gates, w_gate, w_up, w_down):
    tok, share = tokens.shape
    top = expert_ids.shape[1]
    local, width, ff = w_gate.shape
    n_dp = lax.axis_size("dp")
    n_t = lax.axis_size("tensor")
    experts = local * n_dp
    cap = max(2, tok * top * 5 // (4 * experts))
    rows = experts * cap
    per_dev = local * cap
    per = share // BLK
    pw = BLK
    qw = share - pw
    nq = qw // BLK
    nx = nq - 1
    qx = nx * BLK
    px = share - qx
    at = lax.axis_index("tensor").astype(jnp.int32).reshape(1)

    def shift(v, s):
        return lax.ppermute(v, "tensor", [(k, (k + s) % n_t) for k in range(n_t)])

    eye_e = jnp.arange(experts, dtype=jnp.int32)
    hot = expert_ids[:, :, None] == eye_e[None, None, :]
    names = jnp.sum(hot.astype(F32), axis=1)
    gate_of = jnp.sum(jnp.where(hot, gates.astype(F32)[:, :, None], 0.0), axis=1)
    tri = (jnp.arange(tok)[:, None] > jnp.arange(tok)[None, :]).astype(BF)
    slot = jnp.dot(tri, names.astype(BF), preferred_element_type=F32)
    slot = jnp.where(names > 0, slot, -1.0)
    row_id = jnp.arange(rows, dtype=jnp.int32)
    spread = (row_id[:, None] // cap == eye_e[None, :]).astype(BF)
    slot_rows = lax.dot_general(spread, slot.astype(BF), NT, preferred_element_type=F32)
    gate_rows = lax.dot_general(spread, gate_of.astype(BF), NT, preferred_element_type=F32)
    placed = slot_rows == (row_id % cap).astype(F32)[:, None]
    place = placed.astype(BF)
    place_g = jnp.where(placed, gate_rows, 0.0).astype(BF)

    def over_dp(v):
        v = v.reshape(n_dp, per_dev, v.shape[1])
        return lax.all_to_all(v, "dp", 0, 0, tiled=True).reshape(rows, v.shape[2])

    def rows_of(matrix, v):
        return jnp.dot(matrix, v, preferred_element_type=F32).astype(BF)

    def after(v, *done):
        return lax.optimization_barrier((v, *done))

    tail = jnp.concatenate([tokens[:, qx:], cotangent[:, qw:]], axis=1)
    tails = [tail] + [shift(tail, -s) for s in range(1, n_t)]
    tail_x = jnp.concatenate([v[:, :px] for v in tails], axis=1)
    tail_d = jnp.concatenate([v[:, px:] for v in tails], axis=1)
    x0 = over_dp(rows_of(place, tokens[:, :qx]))
    sent, x0, tail_x, tail_d = after(rows_of(place_g, cotangent[:, :qw]), x0, tail_x, tail_d)
    xq = lax.all_gather(x0, "tensor", axis=0)
    d0 = over_dp(sent)
    sent, d0 = after(rows_of(place, tail_x), d0)
    dq = lax.all_gather(d0, "tensor", axis=0)
    xp = over_dp(sent)
    sent, xp = after(rows_of(place_g, tail_d), xp)
    dp = over_dp(sent)

    flops = 2 * 2 * rows * width * ff
    row_bytes = rows * width * 2
    w_bytes = local * width * ff * 2
    chunk = BLK
    row_spec = lambda w: pl.BlockSpec((chunk, w), lambda i: (i, 0))
    shape = jax.ShapeDtypeStruct

    def gathered(w):
        return [
            pl.BlockSpec((None, chunk, w), functools.partial(lambda s, i: (s, i, 0), s))
            for s in range(n_t)
        ]

    def places(w):
        return [[(None, s, 0, w)] for s in range(n_t)] + [[(s, 0, w, share - w) for s in range(n_t)]]

    act, act_t, c1, c2 = pl.pallas_call(
        functools.partial(fwd_kernel, places(qx), share, cap),
        grid=(rows // chunk,),
        in_specs=[SMEM] + gathered(qx) + [row_spec(n_t * px), WHOLE, WHOLE],
        out_specs=[
            row_spec(ff),
            pl.BlockSpec((local * ff, chunk), lambda i: (0, i)),
            row_spec(ff),
            row_spec(ff),
        ],
        out_shape=[
            shape((rows, ff), BF),
            shape((local * ff, rows), BF),
            shape((rows, ff), F32),
            shape((rows, ff), F32),
        ],
        compiler_params=params(),
        cost_estimate=cost(2 * flops, row_bytes + 2 * w_bytes),
        name="hidden",
    )(at, *[xq] * n_t, xp, w_gate, w_up)

    dh, q = pl.pallas_call(
        functools.partial(bwd_kernel, places(qw), share, cap),
        grid=(rows // chunk,),
        in_specs=[SMEM] + gathered(qw) + [row_spec(n_t * pw), WHOLE] + [row_spec(ff)] * 3,
        out_specs=[row_spec(4 * ff), row_spec(1)],
        out_shape=[shape((rows, 4 * ff), BF), shape((rows, 1), F32)],
        compiler_params=params(),
        cost_estimate=cost(flops, row_bytes + w_bytes),
        name="hidden_grad",
    )(at, *[dq] * n_t, dp, w_down, act, c1, c2)

    def row_grad(name, dh, steps, w_at, out_spec, out_shape):
        w_spec = pl.BlockSpec((local, BLK, ff), w_at)
        part = n_t * per // steps
        return pl.pallas_call(
            dx_kernel,
            grid_spec=pltpu.PrefetchScalarGridSpec(
                num_scalar_prefetch=1,
                grid=(steps,),
                in_specs=[pl.BlockSpec((rows, 4 * ff), lambda i, ref: (0, 0)), w_spec, w_spec],
                out_specs=out_spec,
            ),
            out_shape=shape(out_shape, BF),
            compiler_params=params(),
            cost_estimate=cost(2 * flops // part, (row_bytes + 2 * w_bytes) // part),
            name=name,
        )(at, dh, w_gate, w_up)

    def shares_grad(name, dh, first, number):
        return row_grad(
            name,
            dh,
            n_t * number,
            lambda i, ref: (0, i // number * per + first + i % number, 0),
            pl.BlockSpec((None, rows, BLK), lambda i, ref: (i // number, 0, i % number)),
            (n_t, rows, number * BLK),
        )

    out_a = shares_grad("row_grad_a", dh, 0, nq - 1)
    dh, out_a = after(dh, out_a)
    p_out = row_grad(
        "row_grad_tail",
        dh,
        n_t,
        lambda i, ref: (0, (ref[0] + i) % n_t * per + nq, 0),
        pl.BlockSpec((rows, BLK), lambda i, ref: (0, i)),
        (rows, n_t * pw),
    )
    dh, p_out = after(dh, p_out)
    out_b = shares_grad("row_grad_b", dh, nq - 1, 1)

    back_p = over_dp(p_out)
    q_back = lax.all_to_all(q.reshape(n_dp, per_dev), "dp", 0, 0, tiled=True).reshape(rows, 1)
    sum_a = lax.psum_scatter(out_a, "tensor", scatter_dimension=0)

    grads = None
    for s in range(n_t):
        w_spec = pl.BlockSpec((local, BLK, ff), lambda i, ref: (0, (ref[0] + s) % n_t * per + i, 0))
        wd_spec = pl.BlockSpec((local, ff, BLK), lambda i, ref: (0, 0, (ref[0] + s) % n_t * per + i))
        def q_spec(n):
            return pl.BlockSpec(
                (None, rows, BLK), lambda i, ref: ((ref[0] + s) % n_t, 0, jnp.minimum(i, n - 1))
            )

        def p_spec(n):
            return pl.BlockSpec(
                (rows, BLK), lambda i, ref: (0, s * (per - n) + jnp.maximum(i - n, 0))
            )

        given = [xq, xp, dq, dp, dh, act_t]
        before = [] if grads is None else list(grads)
        if s == n_t - 1:
            out_b, sum_a, back_p, q_back, *before = after(out_b, sum_a, back_p, q_back, *before)
            back_a = over_dp(sum_a)
            back_b = over_dp(lax.psum_scatter(out_b, "tensor", scatter_dimension=0))
        grads = pl.pallas_call(
            functools.partial(grad_kernel, nx, nq),
            grid_spec=pltpu.PrefetchScalarGridSpec(
                num_scalar_prefetch=1,
                grid=(per,),
                in_specs=[q_spec(nx), p_spec(nx), q_spec(nq), p_spec(nq)]
                + [
                    pl.BlockSpec((rows, 4 * ff), lambda i, ref: (0, 0)),
                    pl.BlockSpec((local * ff, rows), lambda i, ref: (0, 0)),
                ]
                + [pl.BlockSpec(memory_space=pl.ANY)] * len(before),
                out_specs=[w_spec, w_spec, wd_spec],
            ),
            out_shape=[shape(w_gate.shape, BF), shape(w_up.shape, BF), shape(w_down.shape, BF)],
            input_output_aliases={1 + len(given) + k: k for k in range(len(before))},
            compiler_params=params(),
            cost_estimate=cost(3 * flops // n_t, (2 * row_bytes + 3 * w_bytes) // n_t),
            name="weight_grads",
        )(at, *given, *before)
    grad_gate, grad_up, grad_down = grads

    q_of = lax.dot_general(
        place, (spread.astype(F32) * q_back).astype(BF), TN, preferred_element_type=F32
    )
    q_of = jnp.sum(jnp.where(hot, q_of[:, None, :], 0.0), axis=2)
    tok_p = lax.dot_general(place, back_p, TN, preferred_element_type=F32)
    tail_sum, q_sum = tok_p[:, :pw], q_of
    for s in range(1, n_t):
        both = jnp.concatenate(
            [tok_p[:, s * pw:(s + 1) * pw], jnp.pad(q_of, ((0, 0), (0, 128 - top)))], axis=1
        )
        both = shift(both, s)
        tail_sum, q_sum = tail_sum + both[:, :pw], q_sum + both[:, pw:pw + top]
    grad_gates = (q_sum / gates.astype(F32)).astype(BF)
    tok_a = lax.dot_general(place, back_a, TN, preferred_element_type=F32).astype(BF)
    tok_b = lax.dot_general(place, back_b, TN, preferred_element_type=F32).astype(BF)
    grad_tokens = jnp.concatenate([tok_a, tok_b, tail_sum.astype(BF)], axis=1)
    return grad_tokens, grad_gates, grad_gate, grad_up, grad_down


def solution(mesh):
    in_specs = (
        P("dp", "tensor"),
        P("dp", "tensor"),
        P("dp", None),
        P("dp", None),
        P("dp", None, "tensor"),
        P("dp", None, "tensor"),
        P("dp", "tensor", None),
    )
    out_specs = (
        P("dp", "tensor"),
        P("dp", None),
        P("dp", None, "tensor"),
        P("dp", None, "tensor"),
        P("dp", "tensor", None),
    )
    return jax.shard_map(body, mesh=mesh, in_specs=in_specs, out_specs=out_specs, check_vma=False)
```

time: 795 us -> 343 us (0.43)
  waiting for transfers between devices: 330 us -> 146 us
  local copies, waits for them, and re-layouts: 187 us -> 7.42 us
  matrix products: 124 us -> 14.8 us
  Pallas kernels: 0 us -> 92.3 us
  other arithmetic: 36.3 us -> 3.32 us
  starting transfers between devices: 87.8 us -> 63.9 us
  blocking collectives: 8.56 us -> 0 us
    all_to_all x5 -> x8, waiting for transfers between devices: 245 us -> 119 us  [the longest x7 119 us: over_dp(): return lax.all_to_all(v, 'dp', 0, 0, tiled=True).reshape(rows, v.shape[2])]
    dot_general x9 -> x10, matrix products: 124 us -> 14.8 us  [the longest x4 10.6 us: rows_of(): return jnp.dot(matrix, v, preferred_element_type=F32).astype(BF)]
    pallas_call x0 -> x9, Pallas kernels: none -> 92.3 us  [the longest x4 37.1 us: body(): pl.pallas_call(functools.partial(grad_kernel, nx, nq), grid_spec=pltpu.Pr...]
    all_to_all x4 -> x2, local copies, waits for them, and re-layouts: 50.9 us -> 1.21 us  [body(): lax.all_to_all(q.reshape(n_dp, per_dev), 'dp', 0, 0, tiled=True)]
    reduce_scatter x1 -> x2, waiting for transfers between devices: 58.3 us -> 14.5 us  [the longest x1 14.5 us: body(): back_b = over_dp(lax.psum_scatter(out_b, 'tensor', scatter_dimension=0))]
    scatter x3 -> x0, local copies, waits for them, and re-layouts: 42.9 us -> none  [place_rows(): jnp.zeros((total_rows,) + shape_rest, values.dtype).at[position].set(values)]
    convert_element_type x4 -> x0, local copies, waits for them, and re-layouts: 39.7 us -> none  [the longest x2 39.6 us: body(): dy_rows.astype(jnp.float32)]
    reshape x8 -> x1, local copies, waits for them, and re-layouts: 32.4 us -> 0.09 us  [body(): lax.all_to_all(q.reshape(n_dp, per_dev), 'dp', 0, 0, tiled=True)]
  transfers between devices with their start and end apart: 8 -> 18, of which waited for: 4 -> 10; matrix products, arithmetic and copies ran while one was open for 27% -> 4% of each run, Pallas kernels for 0% -> 20%
where the time goes in v2:
time: 343 us; the launch traced here: 342 us
  waiting for transfers between devices  146 us (43%)
  Pallas kernels  92.3 us (27%)
  starting transfers between devices  63.9 us (19%)
  matrix products  14.8 us (4%)
  between operations  14.1 us (4%)
  local copies, waits for them, and re-layouts  7.42 us (2%)
    all_to_all x7, waiting for transfers between devices, over_dp(): return lax.all_to_all(v, 'dp', 0, 0, tiled=True).reshape(rows, v.shape[2])  119 us
    all_to_all x7, starting transfers between devices, over_dp(): return lax.all_to_all(v, 'dp', 0, 0, tiled=True).reshape(rows, v.shape[2])  50.6 us
    pallas_call x4, Pallas kernels, body(): pl.pallas_call(functools.partial(grad_kernel, nx, nq), grid_spec=pltpu.Pr...  37.1 us
    pallas_call x3, Pallas kernels, row_grad(): pl.pallas_call(dx_kernel, grid_spec=pltpu.PrefetchScalarGridSpec(num_scal...  25.4 us
    pallas_call x1, Pallas kernels, body(): pl.pallas_call(functools.partial(fwd_kernel, places(qx), share, cap), gri...  17.6 us
    reduce_scatter x1, waiting for transfers between devices, body(): back_b = over_dp(lax.psum_scatter(out_b, 'tensor', scatter_dimension=0))  14.5 us
    ppermute x6, waiting for transfers between devices, shift(): return lax.ppermute(v, 'tensor', [(k, (k + s) % n_t) for k in range(n_t)])  12.6 us
    pallas_call x1, Pallas kernels, body(): pl.pallas_call(functools.partial(bwd_kernel, places(qw), share, cap), gri...  12.2 us
  transfers between devices with their start and end apart: 18, of which 10 were waited for; matrix products, arithmetic and copies ran while one was open for 4% of the time, Pallas kernels for 20%

profile of v2, /device:TPU:1, one launch (start us, length us, event | category | flops | bytes accessed | tf_op | source)
XLA Modules:
  0.0 341.7 jit_solution(3098647094995731480)
XLA Ops:
  11.5 9.6 %all-to-all-start = ((bf16[32,40,512]{2,1,0:T(8,128)(2,1)}), bf16[32,40,512]{2,1,0:T(8,128)(2,1)S(1)}, u32[]{:S(2)}, u32[]{:S(2)}) async-start(bf16[32,40,512]{2,1,0:T(8,128)(2,1)} %bitcast.1), calls=%async_computation | async-start | bytes 2621440 | tf_op jit(solution)/shard_map/all_to_all | solution.py:154
  28.8 5.2 %collective-permute-done.1 = bf16[128,768]{1,0:T(8,128)(2,1)S(1)} collective-permute-done((bf16[128,768]{1,0:T(8,128)(2,1)S(1)}, bf16[128,768]{1,0:T(8,128)(2,1)S(1)}, u32[]{:S(2)}, u32[]{:S(2)}) %collective-permute-start.1) | collective-permute-done | bytes 196640 | tf_op jit(solution)/shard_map/ppermute | solution.py:135
  34.2 6.8 %all-to-all-done = bf16[32,40,512]{2,1,0:T(8,128)(2,1)S(1)} async-done(((bf16[32,40,512]{2,1,0:T(8,128)(2,1)}), bf16[32,40,512]{2,1,0:T(8,128)(2,1)S(1)}, u32[]{:S(2)}, u32[]{:S(2)}) %all-to-all-start) | async-done | bytes 1310752 | tf_op jit(solution)/shard_map/all_to_all | solution.py:154
  50.0 23.0 %all-to-all-done.1 = bf16[32,40,768]{2,1,0:T(8,128)(2,1)S(1)} async-done(((bf16[32,40,768]{2,1,0:T(8,128)(2,1)}), bf16[32,40,768]{2,1,0:T(8,128)(2,1)S(1)}, u32[]{:S(2)}, u32[]{:S(2)}) %all-to-all-start.1) | async-done | bytes 1966112 | tf_op jit(solution)/shard_map/all_to_all | solution.py:154
  74.4 5.3 %all-to-all-start.2 = ((bf16[32,40,2048]{2,1,0:T(8,128)(2,1)}), bf16[32,40,2048]{2,1,0:T(8,128)(2,1)}, u32[]{:S(2)}, u32[]{:S(2)}) async-start(bf16[32,40,2048]{2,1,0:T(8,128)(2,1)} %bitcast.54), calls=%async_computation.2 | async-start | bytes 10485760 | tf_op jit(solution)/shard_map/all_to_all | solution.py:154
  82.0 62.3 %all-to-all-done.2 = bf16[32,40,2048]{2,1,0:T(8,128)(2,1)} async-done(((bf16[32,40,2048]{2,1,0:T(8,128)(2,1)}), bf16[32,40,2048]{2,1,0:T(8,128)(2,1)}, u32[]{:S(2)}, u32[]{:S(2)}) %all-to-all-start.2) | async-done | bytes 5242912 | tf_op jit(solution)/shard_map/all_to_all | solution.py:154
  144.3 8.9 %all-to-all-start.3 = ((bf16[32,40,1024]{2,1,0:T(8,128)(2,1)}), bf16[32,40,1024]{2,1,0:T(8,128)(2,1)S(1)}, u32[]{:S(2)}, u32[]{:S(2)}) async-start(bf16[32,40,1024]{2,1,0:T(8,128)(2,1)} %bitcast.56), calls=%async_computation.3 | async-start | bytes 5242880 | tf_op jit(solution)/shard_map/all_to_all | solution.py:154
  153.3 17.6 %hidden.1 = (bf16[1280,256]{1,0:T(8,128)(2,1)}, bf16[512,1280]{1,0:T(8,128)(2,1)}, f32[1280,256]{1,0:T(8,128)}, f32[1280,256]{1,0:T(8,128)}) custom-call(s32[1]{0:T(128)} %bitcast.at, bf16[4,1280,512]{2,1,0:T(8,128)(2,1)} %bitcast.46, bf16[4,1280,512]{2,1,0:T(8,128)(2,1)} %bitcast.47, bf16[4,1280,512]{2,1,0:T(8,128)(2,1)} %bitcast.48, ...), custom_call_target="tpu_custom_call" | custom-call | flops 10737418240 | bytes 18874368 | tf_op jit(solution)/shard_map/hidden/pallas_call | solution.py:192
  170.9 16.2 %all-to-all-done.3 = bf16[32,40,1024]{2,1,0:T(8,128)(2,1)S(1)} async-done(((bf16[32,40,1024]{2,1,0:T(8,128)(2,1)}), bf16[32,40,1024]{2,1,0:T(8,128)(2,1)S(1)}, u32[]{:S(2)}, u32[]{:S(2)}) %all-to-all-start.3) | async-done | bytes 2621472 | tf_op jit(solution)/shard_map/all_to_all | solution.py:154
  188.7 12.2 %hidden_grad.1 = (bf16[1280,1024]{1,0:T(8,128)(2,1)}, f32[1280,1]{1,0:T(8,128)}) custom-call(s32[1]{0:T(128)} %bitcast.at, bf16[4,1280,768]{2,1,0:T(8,128)(2,1)} %bitcast.33, bf16[4,1280,768]{2,1,0:T(8,128)(2,1)} %bitcast.34, bf16[4,1280,768]{2,1,0:T(8,128)(2,1)} %bitcast.35, bf16[4,1280,768]{2,1,0:T(8,128)(2,1)} %bitcast.36, bf16[1280,1024]{1,0:T(8,128)(2,1)} %bitcast.41, ...), custom_call_target="tpu_custom_call" | custom-call | flops 5368709120 | bytes 14680064 | tf_op jit(solution)/shard_map/hidden_grad/pallas_call | solution.py:213
  200.9 11.2 %row_grad_a.1 = bf16[4,1280,512]{2,1,0:T(8,128)(2,1)} custom-call(s32[1]{0:T(128)} %bitcast.at, bf16[1280,1024]{1,0:T(8,128)(2,1)} %get-tuple-element.55.dh, bf16[2,4096,256]{2,1,0:T(8,128)(2,1)} %wg.5, bf16[2,4096,256]{2,1,0:T(8,128)(2,1)} %wu.5), custom_call_target="tpu_custom_call" | custom-call | flops 5368709120 | bytes 9437184 | tf_op jit(solution)/shard_map/row_grad_a/pallas_call | solution.py:227
  214.2 4.6 %all-to-all-start.5 = ((f32[32,1,40]{2,1,0:T(1,128)}), f32[32,1,40]{2,1,0:T(1,128)S(1)}, u32[]{:S(2)}, u32[]{:S(2)}) async-start(f32[32,1,40]{2,1,0:T(1,128)} %bitcast.14), calls=%async_computation.6 | async-start | bytes 32768 | tf_op jit(solution)/shard_map/all_to_all | solution.py:265
  218.8 7.4 %row_grad_tail.1 = bf16[1280,1024]{1,0:T(8,128)(2,1)} custom-call(s32[1]{0:T(128)} %bitcast.at, bf16[1280,1024]{1,0:T(8,128)(2,1)} %get-tuple-element.55.dh, bf16[2,4096,256]{2,1,0:T(8,128)(2,1)} %wg.5, bf16[2,4096,256]{2,1,0:T(8,128)(2,1)} %wu.5), custom_call_target="tpu_custom_call" | custom-call | flops 2684354560 | bytes 4718592 | tf_op jit(solution)/shard_map/row_grad_tail/pallas_call | solution.py:227
  226.2 7.5 %all-to-all-start.4 = ((bf16[32,40,1024]{2,1,0:T(8,128)(2,1)}), bf16[32,40,1024]{2,1,0:T(8,128)(2,1)S(1)}, u32[]{:S(2)}, u32[]{:S(2)}) async-start(bf16[32,40,1024]{2,1,0:T(8,128)(2,1)} %bitcast.57), calls=%async_computation.5 | async-start | bytes 5242880 | tf_op jit(solution)/shard_map/all_to_all | solution.py:154
  233.8 6.8 %row_grad_b.1 = bf16[4,1280,256]{2,1,0:T(8,128)(2,1)} custom-call(s32[1]{0:T(128)} %bitcast.at, bf16[1280,1024]{1,0:T(8,128)(2,1)} %get-tuple-element.55.dh, bf16[2,4096,256]{2,1,0:T(8,128)(2,1)} %wg.5, bf16[2,4096,256]{2,1,0:T(8,128)(2,1)} %wu.5), custom_call_target="tpu_custom_call" | custom-call | flops 2684354560 | bytes 4718592 | tf_op jit(solution)/shard_map/row_grad_b/pallas_call | solution.py:227
  240.6 9.3 %weight_grads.4 = (bf16[2,4096,256]{2,1,0:T(8,128)(2,1)}, bf16[2,4096,256]{2,1,0:T(8,128)(2,1)}, bf16[2,256,4096]{2,1,0:T(8,128)(2,1)}) custom-call(s32[1]{0:T(128)} %bitcast.at, bf16[4,1280,512]{2,1,0:T(8,128)(2,1)} %bitcast.50, bf16[1280,2048]{1,0:T(8,128)(2,1)} %bitcast.7.refs_4_.xp, bf16[4,1280,768]{2,1,0:T(8,128)(2,1)} %bitcast.37, ...), custom_call_target="tpu_custom_call" | custom-call | flops 4026531840 | bytes 8388608 | tf_op jit(solution)/shard_map/weight_grads/pallas_call | solution.py:288
  249.9 9.3 %weight_grads.5 = (bf16[2,4096,256]{2,1,0:T(8,128)(2,1)}, bf16[2,4096,256]{2,1,0:T(8,128)(2,1)}, bf16[2,256,4096]{2,1,0:T(8,128)(2,1)}) custom-call(s32[1]{0:T(128)} %bitcast.at, bf16[4,1280,512]{2,1,0:T(8,128)(2,1)} %bitcast.51, bf16[1280,2048]{1,0:T(8,128)(2,1)} %bitcast.7.refs_4_.xp, ...), custom_call_target="tpu_custom_call", output_to_operand_aliasing={{0}: (7, {}), {1}: (8, {}), {2}: (9, {})} | custom-call | flops 4026531840 | bytes 8388608 | tf_op jit(solution)/shard_map/weight_grads/pallas_call | solution.py:288
  259.2 9.3 %weight_grads.6 = (bf16[2,4096,256]{2,1,0:T(8,128)(2,1)}, bf16[2,4096,256]{2,1,0:T(8,128)(2,1)}, bf16[2,256,4096]{2,1,0:T(8,128)(2,1)}) custom-call(s32[1]{0:T(128)} %bitcast.at, bf16[4,1280,512]{2,1,0:T(8,128)(2,1)} %bitcast.52, bf16[1280,2048]{1,0:T(8,128)(2,1)} %bitcast.7.refs_4_.xp, ...), custom_call_target="tpu_custom_call", output_to_operand_aliasing={{0}: (7, {}), {1}: (8, {}), {2}: (9, {})} | custom-call | flops 4026531840 | bytes 8388608 | tf_op jit(solution)/shard_map/weight_grads/pallas_call | solution.py:288
  269.9 7.5 %all-to-all-start.6 = ((bf16[32,40,512]{2,1,0:T(8,128)(2,1)}), bf16[32,40,512]{2,1,0:T(8,128)(2,1)}, u32[]{:S(2)}, u32[]{:S(2)}) async-start(bf16[32,40,512]{2,1,0:T(8,128)(2,1)} %bitcast.62), calls=%async_computation.7 | async-start | bytes 2621440 | tf_op jit(solution)/shard_map/all_to_all | solution.py:154
  282.5 9.2 %weight_grads.7 = (bf16[2,4096,256]{2,1,0:T(8,128)(2,1)}, bf16[2,4096,256]{2,1,0:T(8,128)(2,1)}, bf16[2,256,4096]{2,1,0:T(8,128)(2,1)}) custom-call(s32[1]{0:T(128)} %bitcast.at, bf16[4,1280,512]{2,1,0:T(8,128)(2,1)} %bitcast.53, bf16[1280,2048]{1,0:T(8,128)(2,1)} %bitcast.7.refs_4_.xp, ...), custom_call_target="tpu_custom_call", output_to_operand_aliasing={{0}: (7, {}), {1}: (8, {}), {2}: (9, {})} | custom-call | flops 4026531840 | bytes 8388608 | tf_op jit(solution)/shard_map/weight_grads/pallas_call | solution.py:288
  293.8 5.1 %collective-permute-done.3 = f32[128,384]{1,0:T(8,128)S(1)} collective-permute-done((f32[128,384]{1,0:T(8,128)S(1)}, f32[128,384]{1,0:T(8,128)S(1)}, u32[]{:S(2)}, u32[]{:S(2)}) %collective-permute-start.3) | collective-permute-done | bytes 196640 | tf_op jit(solution)/shard_map/ppermute | solution.py:135
  299.0 14.5 %reduce-scatter.5.cloned.1.call-done = bf16[1,1280,256]{2,1,0:T(8,128)(2,1)} async-done(((bf16[4,1280,256]{2,1,0:T(8,128)(2,1)}), bf16[1,1280,256]{2,1,0:T(8,128)(2,1)}) %reduce-scatter.5.cloned.1.call-update) | async-done | bytes 655376 | tf_op jit(solution)/shard_map/reduce_scatter | solution.py:287
  313.4 7.7 %all-to-all-start.7 = ((bf16[32,40,256]{2,1,0:T(8,128)(2,1)}), bf16[32,40,256]{2,1,0:T(8,128)(2,1)S(1)}, u32[]{:S(2)}, u32[]{:S(2)}) async-start(bf16[32,40,256]{2,1,0:T(8,128)(2,1)} %bitcast.63), calls=%async_computation.9 | async-start | bytes 1310720 | tf_op jit(solution)/shard_map/all_to_all | solution.py:154
  323.6 10.4 %all-to-all-done.7 = bf16[32,40,256]{2,1,0:T(8,128)(2,1)S(1)} async-done(((bf16[32,40,256]{2,1,0:T(8,128)(2,1)}), bf16[32,40,256]{2,1,0:T(8,128)(2,1)S(1)}, u32[]{:S(2)}, u32[]{:S(2)}) %all-to-all-start.7) | async-done | bytes 655392 | tf_op jit(solution)/shard_map/all_to_all | solution.py:154
  (86 shorter events, 40.7 us)
Async XLA Ops:
  8.6 12.6 %copy-start.5 = (bf16[128,1024]{1,0:T(8,128)(2,1)S(1)}, bf16[128,1024]{1,0:T(8,128)(2,1)}, u32[]{:S(2)}) copy-start(bf16[128,1024]{1,0:T(8,128)(2,1)} %param.7) | copy-start | bytes 786436
  8.6 12.6 %copy-start.4 = (bf16[128,1024]{1,0:T(8,128)(2,1)S(1)}, bf16[128,1024]{1,0:T(8,128)(2,1)}, u32[]{:S(2)}) copy-start(bf16[128,1024]{1,0:T(8,128)(2,1)} %param.8) | copy-start | bytes 786436
  11.5 29.4 %all-to-all-start = ((bf16[32,40,512]{2,1,0:T(8,128)(2,1)}), bf16[32,40,512]{2,1,0:T(8,128)(2,1)S(1)}, u32[]{:S(2)}, u32[]{:S(2)}) async-start(bf16[32,40,512]{2,1,0:T(8,128)(2,1)} %bitcast.1), calls=%async_computation | async-start | bytes 2621440 | tf_op jit(solution)/shard_map/all_to_all | solution.py:154
  21.1 132.2 %all-gather.7.cloned.1.call-start = ((), (), s32[]{:S(2)}) async-start(), calls=%async_computation.13 | async-start | bytes 6553600 | tf_op jit(solution)/shard_map/all_gather | solution.py:168
  21.3 7.5 %collective-permute-start.2 = (bf16[128,768]{1,0:T(8,128)(2,1)S(1)}, bf16[128,768]{1,0:T(8,128)(2,1)S(1)}, u32[]{:S(2)}, u32[]{:S(2)}) collective-permute-start(bf16[128,768]{1,0:T(8,128)(2,1)S(1)} %pad_maximum_fusion.3), channel_id=1, source_target_pairs={{0,1},{1,2},{2,3},{3,0},{4,5},{5,6},{6,7},{7,4},{8,9},{9,10},{10,1... | collective-permute-start | bytes 589832 | tf_op jit(solution)/shard_map/ppermute | solution.py:135
  22.6 11.5 %collective-permute-start.1 = (bf16[128,768]{1,0:T(8,128)(2,1)S(1)}, bf16[128,768]{1,0:T(8,128)(2,1)S(1)}, u32[]{:S(2)}, u32[]{:S(2)}) collective-permute-start(bf16[128,768]{1,0:T(8,128)(2,1)S(1)} %pad_maximum_fusion.3), channel_id=1, source_target_pairs={{0,2},{1,3},{2,0},{3,1},{4,6},{5,7},{6,4},{7,5},{8,10},{9,11},{10,... | collective-permute-start | bytes 589832 | tf_op jit(solution)/shard_map/ppermute | solution.py:135
  25.0 9.0 %collective-permute-start = (bf16[128,768]{1,0:T(8,128)(2,1)S(1)}, bf16[128,768]{1,0:T(8,128)(2,1)S(1)}, u32[]{:S(2)}, u32[]{:S(2)}) collective-permute-start(bf16[128,768]{1,0:T(8,128)(2,1)S(1)} %pad_maximum_fusion.3), channel_id=1, source_target_pairs={{0,3},{1,0},{2,1},{3,2},{4,7},{5,4},{6,5},{7,6},{8,11},{9,8},{10,9... | collective-permute-start | bytes 589832 | tf_op jit(solution)/shard_map/ppermute | solution.py:135
  42.0 31.0 %all-to-all-start.1 = ((bf16[32,40,768]{2,1,0:T(8,128)(2,1)}), bf16[32,40,768]{2,1,0:T(8,128)(2,1)S(1)}, u32[]{:S(2)}, u32[]{:S(2)}) async-start(bf16[32,40,768]{2,1,0:T(8,128)(2,1)} %bitcast.59), calls=%async_computation.1 | async-start | bytes 3932160 | tf_op jit(solution)/shard_map/all_to_all | solution.py:154
  46.1 141.0 %all-gather.5.cloned.1.call-start = ((), (), s32[]{:S(2)}) async-start(), calls=%async_computation.12 | async-start | bytes 9830400 | tf_op jit(solution)/shard_map/all_gather | solution.py:171
  73.1 1.3 copy-start.1
  74.4 70.0 %all-to-all-start.2 = ((bf16[32,40,2048]{2,1,0:T(8,128)(2,1)}), bf16[32,40,2048]{2,1,0:T(8,128)(2,1)}, u32[]{:S(2)}, u32[]{:S(2)}) async-start(bf16[32,40,2048]{2,1,0:T(8,128)(2,1)} %bitcast.54), calls=%async_computation.2 | async-start | bytes 10485760 | tf_op jit(solution)/shard_map/all_to_all | solution.py:154
  144.3 42.8 %all-to-all-start.3 = ((bf16[32,40,1024]{2,1,0:T(8,128)(2,1)}), bf16[32,40,1024]{2,1,0:T(8,128)(2,1)S(1)}, u32[]{:S(2)}, u32[]{:S(2)}) async-start(bf16[32,40,1024]{2,1,0:T(8,128)(2,1)} %bitcast.56), calls=%async_computation.3 | async-start | bytes 5242880 | tf_op jit(solution)/shard_map/all_to_all | solution.py:154
  153.2 116.6 %reduce-scatter.3.cloned.1.call-start = ((), (), s32[]{:S(2)}) async-start(), calls=%async_computation.10 | async-start | bytes 6553600 | tf_op jit(solution)/shard_map/reduce_scatter | solution.py:266
  187.1 1.6 copy-start
  214.2 12.0 %all-to-all-start.5 = ((f32[32,1,40]{2,1,0:T(1,128)}), f32[32,1,40]{2,1,0:T(1,128)S(1)}, u32[]{:S(2)}, u32[]{:S(2)}) async-start(f32[32,1,40]{2,1,0:T(1,128)} %bitcast.14), calls=%async_computation.6 | async-start | bytes 32768 | tf_op jit(solution)/shard_map/all_to_all | solution.py:265
  226.2 43.6 %all-to-all-start.4 = ((bf16[32,40,1024]{2,1,0:T(8,128)(2,1)}), bf16[32,40,1024]{2,1,0:T(8,128)(2,1)S(1)}, u32[]{:S(2)}, u32[]{:S(2)}) async-start(bf16[32,40,1024]{2,1,0:T(8,128)(2,1)} %bitcast.57), calls=%async_computation.5 | async-start | bytes 5242880 | tf_op jit(solution)/shard_map/all_to_all | solution.py:154
  233.7 79.7 %reduce-scatter.5.cloned.1.call-start = ((), (), s32[]{:S(2)}) async-start(), calls=%async_computation.11 | async-start | bytes 3276800 | tf_op jit(solution)/shard_map/reduce_scatter | solution.py:287
  269.8 8.3 %copy-start.6 = (s32[128,8]{0,1:T(8,128)S(1)}, s32[128,8]{0,1:T(8,128)}, u32[]{:S(2)}) copy-start(s32[128,8]{0,1:T(8,128)} %param.9) | copy-start | bytes 12292
  269.9 29.1 %all-to-all-start.6 = ((bf16[32,40,512]{2,1,0:T(8,128)(2,1)}), bf16[32,40,512]{2,1,0:T(8,128)(2,1)}, u32[]{:S(2)}, u32[]{:S(2)}) async-start(bf16[32,40,512]{2,1,0:T(8,128)(2,1)} %bitcast.62), calls=%async_computation.7 | async-start | bytes 2621440 | tf_op jit(solution)/shard_map/all_to_all | solution.py:154
  278.9 12.8 %collective-permute-start.5 = (f32[128,384]{1,0:T(8,128)S(1)}, f32[128,384]{1,0:T(8,128)S(1)}, u32[]{:S(2)}, u32[]{:S(2)}) collective-permute-start(f32[128,384]{1,0:T(8,128)S(1)} %get-tuple-element.106), channel_id=1, source_target_pairs={{0,3},{1,0},{2,1},{3,2},{4,7},{5,4},{6,5},{7,6},{8,11},{9,8},{10,9... | collective-permute-start | bytes 589832 | tf_op jit(solution)/shard_map/ppermute | solution.py:135
  281.4 12.4 %collective-permute-start.4 = (f32[128,384]{1,0:T(8,128)S(1)}, f32[128,384]{1,0:T(8,128)S(1)}, u32[]{:S(2)}, u32[]{:S(2)}) collective-permute-start(f32[128,384]{1,0:T(8,128)S(1)} %get-tuple-element.105), channel_id=1, source_target_pairs={{0,2},{1,3},{2,0},{3,1},{4,6},{5,7},{6,4},{7,5},{8,10},{9,11},{10,... | collective-permute-start | bytes 589832 | tf_op jit(solution)/shard_map/ppermute | solution.py:135
  281.9 39.2 %copy-start.7 = (bf16[128,8]{0,1:T(8,128)(2,1)S(1)}, bf16[128,8]{0,1:T(8,128)(2,1)}, u32[]{:S(2)}) copy-start(bf16[128,8]{0,1:T(8,128)(2,1)} %param.10) | copy-start | bytes 6148
  281.9 17.0 %collective-permute-start.3 = (f32[128,384]{1,0:T(8,128)S(1)}, f32[128,384]{1,0:T(8,128)S(1)}, u32[]{:S(2)}, u32[]{:S(2)}) collective-permute-start(f32[128,384]{1,0:T(8,128)S(1)} %get-tuple-element.104), channel_id=1, source_target_pairs={{0,1},{1,2},{2,3},{3,0},{4,5},{5,6},{6,7},{7,4},{8,9},{9,10},{10,1... | collective-permute-start | bytes 589832 | tf_op jit(solution)/shard_map/ppermute | solution.py:135
  313.4 20.6 %all-to-all-start.7 = ((bf16[32,40,256]{2,1,0:T(8,128)(2,1)}), bf16[32,40,256]{2,1,0:T(8,128)(2,1)S(1)}, u32[]{:S(2)}, u32[]{:S(2)}) async-start(bf16[32,40,256]{2,1,0:T(8,128)(2,1)} %bitcast.63), calls=%async_computation.9 | async-start | bytes 1310720 | tf_op jit(solution)/shard_map/all_to_all | solution.py:154
  (2 other events, 2.1 us)
Sparse Core Ops, SparseCore 0:
  42.1 54.4 all-gather.6
  98.8 79.1 all-gather.4
  212.3 53.1 reduce-scatter.2
  270.0 43.4 reduce-scatter.4

commit v3 on v2

--- a/solution.py
+++ b/solution.py
@@ -61,8 +61,7 @@
     c1[...] = h2 * s * (1.0 + h1 * (1.0 - s))
 
 
-def bwd_kernel(places, share, cap, at, *refs):
-    ds, (wd, act, c1, c2, dh, q) = refs[:-6], refs[-6:]
+def da_terms(places, share, cap, at, ds, wd):
     rows = ds[0].shape[0]
     sums = [None] * 2
     for d, begin, width in pieces(places, share, wd.shape[2] // share, at, ds):
@@ -71,7 +70,18 @@
             term = lax.dot_general(d, w, NT, preferred_element_type=F32)
             sums[e] = term if sums[e] is None else sums[e] + term
     mask = first_expert(pl.program_id(0) * rows, rows, cap)
-    da = jnp.where(mask, sums[0], sums[1])
+    return mask, jnp.where(mask, sums[0], sums[1])
+
+
+def bwd_early_kernel(places, share, cap, at, *refs):
+    ds, (wd, da) = refs[:-2], refs[-2:]
+    da[...] = da_terms(places, share, cap, at, ds, wd)[1]
+
+
+def bwd_kernel(places, share, cap, at, *refs):
+    ds, (wd, early, act, c1, c2, dh, q) = refs[:-7], refs[-7:]
+    mask, da = da_terms(places, share, cap, at, ds, wd)
+    da = da + early[...]
     d1 = da * c1[...]
     d2 = da * c2[...]
     for k, v in enumerate((d1, d2)):
@@ -210,16 +220,26 @@
         name="hidden",
     )(at, *[xq] * n_t, xp, w_gate, w_up)
 
+    early = pl.pallas_call(
+        functools.partial(bwd_early_kernel, places(qw)[:n_t], share, cap),
+        grid=(rows // chunk,),
+        in_specs=[SMEM] + gathered(qw) + [WHOLE],
+        out_specs=row_spec(ff),
+        out_shape=shape((rows, ff), F32),
+        compiler_params=params(),
+        cost_estimate=cost(flops * 3 // 4, row_bytes * 3 // 4 + w_bytes),
+        name="hidden_grad_early",
+    )(at, *[dq] * n_t, w_down)
     dh, q = pl.pallas_call(
-        functools.partial(bwd_kernel, places(qw), share, cap),
+        functools.partial(bwd_kernel, places(qw)[n_t:], share, cap),
         grid=(rows // chunk,),
-        in_specs=[SMEM] + gathered(qw) + [row_spec(n_t * pw), WHOLE] + [row_spec(ff)] * 3,
+        in_specs=[SMEM, row_spec(n_t * pw), WHOLE] + [row_spec(ff)] * 4,
         out_specs=[row_spec(4 * ff), row_spec(1)],
         out_shape=[shape((rows, 4 * ff), BF), shape((rows, 1), F32)],
         compiler_params=params(),
-        cost_estimate=cost(flops, row_bytes + w_bytes),
+        cost_estimate=cost(flops // 4, row_bytes // 4 + w_bytes),
         name="hidden_grad",
-    )(at, *[dq] * n_t, dp, w_down, act, c1, c2)
+    )(at, dp, w_down, early, act, c1, c2)
 
     def row_grad(name, dh, steps, w_at, out_spec, out_shape):
         w_spec = pl.BlockSpec((local, BLK, ff), w_at)

time: 343 us -> 343 us (level)
  waiting for transfers between devices: 146 us -> 137 us
  Pallas kernels: 92.3 us -> 98.3 us
    all_to_all x7, waiting for transfers between devices: 119 us -> 103 us  [over_dp(): return lax.all_to_all(v, 'dp', 0, 0, tiled=True).reshape(rows, v.shape[2])]
    all_gather x1, waiting for transfers between devices: 0.01 us -> 7.2 us  [body(): dq = lax.all_gather(d0, 'tensor', axis=0)]
    pallas_call x1 -> x2, Pallas kernels: 12.2 us -> 18.1 us  [the longest x1 9.49 us: body(): pl.pallas_call(functools.partial(bwd_early_kernel, places(qw)[:n_t], shar...]
  transfers between devices with their start and end apart: 18 -> 18, of which waited for: 10 -> 10; matrix products, arithmetic and copies ran while one was open for 4% -> 4% of each run, Pallas kernels for 20% -> 23%
where the time goes in v3:
time: 343 us; the launch traced here: 342 us
  waiting for transfers between devices  137 us (40%)
  Pallas kernels  98.3 us (29%)
  starting transfers between devices  66.8 us (19%)
  matrix products  14.8 us (4%)
  between operations  14.1 us (4%)
  local copies, waits for them, and re-layouts  7.42 us (2%)
    all_to_all x7, waiting for transfers between devices, over_dp(): return lax.all_to_all(v, 'dp', 0, 0, tiled=True).reshape(rows, v.shape[2])  103 us
    all_to_all x7, starting transfers between devices, over_dp(): return lax.all_to_all(v, 'dp', 0, 0, tiled=True).reshape(rows, v.shape[2])  50.5 us
    pallas_call x4, Pallas kernels, body(): pl.pallas_call(functools.partial(grad_kernel, nx, nq), grid_spec=pltpu.Pr...  37.1 us
    pallas_call x3, Pallas kernels, row_grad(): pl.pallas_call(dx_kernel, grid_spec=pltpu.PrefetchScalarGridSpec(num_scal...  25.5 us
    pallas_call x1, Pallas kernels, body(): pl.pallas_call(functools.partial(fwd_kernel, places(qx), share, cap), gri...  17.6 us
    reduce_scatter x1, waiting for transfers between devices, body(): back_b = over_dp(lax.psum_scatter(out_b, 'tensor', scatter_dimension=0))  14.4 us
    ppermute x6, waiting for transfers between devices, shift(): return lax.ppermute(v, 'tensor', [(k, (k + s) % n_t) for k in range(n_t)])  12.6 us
    dot_general x4, matrix products, rows_of(): return jnp.dot(matrix, v, preferred_element_type=F32).astype(BF)  10.6 us
  transfers between devices with their start and end apart: 18, of which 10 were waited for; matrix products, arithmetic and copies ran while one was open for 4% of the time, Pallas kernels for 23%

profile of v3, /device:TPU:1, one launch (start us, length us, event | category | flops | bytes accessed | tf_op | source)
XLA Modules:
  0.0 341.5 jit_solution(18002012513636165894)
XLA Ops:
  11.5 9.6 %all-to-all-start = ((bf16[32,40,512]{2,1,0:T(8,128)(2,1)}), bf16[32,40,512]{2,1,0:T(8,128)(2,1)S(1)}, u32[]{:S(2)}, u32[]{:S(2)}) async-start(bf16[32,40,512]{2,1,0:T(8,128)(2,1)} %bitcast.1), calls=%async_computation | async-start | bytes 2621440 | tf_op jit(solution)/shard_map/all_to_all | solution.py:164
  34.2 6.8 %all-to-all-done = bf16[32,40,512]{2,1,0:T(8,128)(2,1)S(1)} async-done(((bf16[32,40,512]{2,1,0:T(8,128)(2,1)}), bf16[32,40,512]{2,1,0:T(8,128)(2,1)S(1)}, u32[]{:S(2)}, u32[]{:S(2)}) %all-to-all-start) | async-done | bytes 1310752 | tf_op jit(solution)/shard_map/all_to_all | solution.py:164
  50.0 23.0 %all-to-all-done.1 = bf16[32,40,768]{2,1,0:T(8,128)(2,1)S(1)} async-done(((bf16[32,40,768]{2,1,0:T(8,128)(2,1)}), bf16[32,40,768]{2,1,0:T(8,128)(2,1)S(1)}, u32[]{:S(2)}, u32[]{:S(2)}) %all-to-all-start.1) | async-done | bytes 1966112 | tf_op jit(solution)/shard_map/all_to_all | solution.py:164
  74.4 5.3 %all-to-all-start.2 = ((bf16[32,40,2048]{2,1,0:T(8,128)(2,1)}), bf16[32,40,2048]{2,1,0:T(8,128)(2,1)}, u32[]{:S(2)}, u32[]{:S(2)}) async-start(bf16[32,40,2048]{2,1,0:T(8,128)(2,1)} %bitcast.54), calls=%async_computation.2 | async-start | bytes 10485760 | tf_op jit(solution)/shard_map/all_to_all | solution.py:164
  82.0 62.3 %all-to-all-done.2 = bf16[32,40,2048]{2,1,0:T(8,128)(2,1)} async-done(((bf16[32,40,2048]{2,1,0:T(8,128)(2,1)}), bf16[32,40,2048]{2,1,0:T(8,128)(2,1)}, u32[]{:S(2)}, u32[]{:S(2)}) %all-to-all-start.2) | async-done | bytes 5242912 | tf_op jit(solution)/shard_map/all_to_all | solution.py:164
  144.3 8.9 %all-to-all-start.3 = ((bf16[32,40,1024]{2,1,0:T(8,128)(2,1)}), bf16[32,40,1024]{2,1,0:T(8,128)(2,1)S(1)}, u32[]{:S(2)}, u32[]{:S(2)}) async-start(bf16[32,40,1024]{2,1,0:T(8,128)(2,1)} %bitcast.56), calls=%async_computation.3 | async-start | bytes 5242880 | tf_op jit(solution)/shard_map/all_to_all | solution.py:164
  153.3 17.6 %hidden.1 = (bf16[1280,256]{1,0:T(8,128)(2,1)}, bf16[512,1280]{1,0:T(8,128)(2,1)}, f32[1280,256]{1,0:T(8,128)}, f32[1280,256]{1,0:T(8,128)}) custom-call(s32[1]{0:T(128)} %bitcast.at, bf16[4,1280,512]{2,1,0:T(8,128)(2,1)} %bitcast.46, bf16[4,1280,512]{2,1,0:T(8,128)(2,1)} %bitcast.47, bf16[4,1280,512]{2,1,0:T(8,128)(2,1)} %bitcast.48, ...), custom_call_target="tpu_custom_call" | custom-call | flops 10737418240 | bytes 18874368 | tf_op jit(solution)/shard_map/hidden/pallas_call | solution.py:202
  170.9 7.2 %all-gather.5.cloned.1.call-done = bf16[5120,768]{1,0:T(8,128)(2,1)} async-done(((bf16[1280,768]{1,0:T(8,128)(2,1)}), bf16[5120,768]{1,0:T(8,128)(2,1)}) %all-gather.5.cloned.1.call-update) | async-done | bytes 7864336 | tf_op jit(solution)/shard_map/all_gather | solution.py:181
  178.1 9.5 %hidden_grad_early.1.refs_2_ = f32[1280,256]{1,0:T(8,128)} custom-call(s32[1]{0:T(128)} %bitcast.at, bf16[4,1280,768]{2,1,0:T(8,128)(2,1)} %bitcast.33, bf16[4,1280,768]{2,1,0:T(8,128)(2,1)} %bitcast.34, bf16[4,1280,768]{2,1,0:T(8,128)(2,1)} %bitcast.35, bf16[4,1280,768]{2,1,0:T(8,128)(2,1)} %bitcast.36, bf16[2,256,4096]{2,1,0:T(8,128)(2,1)} %refs_1_.1), custom_call_target="tpu_custom_call" | custom-call | flops 4026531840 | bytes 12058624 | tf_op jit(solution)/shard_map/hidden_grad_early/pallas_call | solution.py:223
  189.2 8.6 %hidden_grad.1 = (bf16[1280,1024]{1,0:T(8,128)(2,1)}, f32[1280,1]{1,0:T(8,128)}) custom-call(s32[1]{0:T(128)} %bitcast.at, bf16[1280,1024]{1,0:T(8,128)(2,1)} %bitcast.41, bf16[2,256,4096]{2,1,0:T(8,128)(2,1)} %refs_1_.1, f32[1280,256]{1,0:T(8,128)} %hidden_grad_early.1.refs_2_, bf16[1280,256]{1,0:T(8,128)(2,1)} %get-tuple-element.50.refs_3_, ...), custom_call_target="tpu_custom_call" | custom-call | flops 1342177280 | bytes 6815744 | tf_op jit(solution)/shard_map/hidden_grad/pallas_call | solution.py:233
  197.8 11.2 %row_grad_a.1 = bf16[4,1280,512]{2,1,0:T(8,128)(2,1)} custom-call(s32[1]{0:T(128)} %bitcast.at, bf16[1280,1024]{1,0:T(8,128)(2,1)} %get-tuple-element.55.dh, bf16[2,4096,256]{2,1,0:T(8,128)(2,1)} %wg.5, bf16[2,4096,256]{2,1,0:T(8,128)(2,1)} %wu.5), custom_call_target="tpu_custom_call" | custom-call | flops 5368709120 | bytes 9437184 | tf_op jit(solution)/shard_map/row_grad_a/pallas_call | solution.py:247
  211.0 7.7 %all-to-all-start.5 = ((f32[32,1,40]{2,1,0:T(1,128)}), f32[32,1,40]{2,1,0:T(1,128)S(1)}, u32[]{:S(2)}, u32[]{:S(2)}) async-start(f32[32,1,40]{2,1,0:T(1,128)} %bitcast.14), calls=%async_computation.6 | async-start | bytes 32768 | tf_op jit(solution)/shard_map/all_to_all | solution.py:285
  218.8 7.4 %row_grad_tail.1 = bf16[1280,1024]{1,0:T(8,128)(2,1)} custom-call(s32[1]{0:T(128)} %bitcast.at, bf16[1280,1024]{1,0:T(8,128)(2,1)} %get-tuple-element.55.dh, bf16[2,4096,256]{2,1,0:T(8,128)(2,1)} %wg.5, bf16[2,4096,256]{2,1,0:T(8,128)(2,1)} %wu.5), custom_call_target="tpu_custom_call" | custom-call | flops 2684354560 | bytes 4718592 | tf_op jit(solution)/shard_map/row_grad_tail/pallas_call | solution.py:247
  226.2 7.5 %all-to-all-start.4 = ((bf16[32,40,1024]{2,1,0:T(8,128)(2,1)}), bf16[32,40,1024]{2,1,0:T(8,128)(2,1)S(1)}, u32[]{:S(2)}, u32[]{:S(2)}) async-start(bf16[32,40,1024]{2,1,0:T(8,128)(2,1)} %bitcast.57), calls=%async_computation.5 | async-start | bytes 5242880 | tf_op jit(solution)/shard_map/all_to_all | solution.py:164
  233.8 6.8 %row_grad_b.1 = bf16[4,1280,256]{2,1,0:T(8,128)(2,1)} custom-call(s32[1]{0:T(128)} %bitcast.at, bf16[1280,1024]{1,0:T(8,128)(2,1)} %get-tuple-element.55.dh, bf16[2,4096,256]{2,1,0:T(8,128)(2,1)} %wg.5, bf16[2,4096,256]{2,1,0:T(8,128)(2,1)} %wu.5), custom_call_target="tpu_custom_call" | custom-call | flops 2684354560 | bytes 4718592 | tf_op jit(solution)/shard_map/row_grad_b/pallas_call | solution.py:247
  240.6 9.3 %weight_grads.4 = (bf16[2,4096,256]{2,1,0:T(8,128)(2,1)}, bf16[2,4096,256]{2,1,0:T(8,128)(2,1)}, bf16[2,256,4096]{2,1,0:T(8,128)(2,1)}) custom-call(s32[1]{0:T(128)} %bitcast.at, bf16[4,1280,512]{2,1,0:T(8,128)(2,1)} %bitcast.50, bf16[1280,2048]{1,0:T(8,128)(2,1)} %bitcast.6.refs_4_.xp, bf16[4,1280,768]{2,1,0:T(8,128)(2,1)} %bitcast.37, ...), custom_call_target="tpu_custom_call" | custom-call | flops 4026531840 | bytes 8388608 | tf_op jit(solution)/shard_map/weight_grads/pallas_call | solution.py:308
  249.9 9.3 %weight_grads.5 = (bf16[2,4096,256]{2,1,0:T(8,128)(2,1)}, bf16[2,4096,256]{2,1,0:T(8,128)(2,1)}, bf16[2,256,4096]{2,1,0:T(8,128)(2,1)}) custom-call(s32[1]{0:T(128)} %bitcast.at, bf16[4,1280,512]{2,1,0:T(8,128)(2,1)} %bitcast.51, bf16[1280,2048]{1,0:T(8,128)(2,1)} %bitcast.6.refs_4_.xp, ...), custom_call_target="tpu_custom_call", output_to_operand_aliasing={{0}: (7, {}), {1}: (8, {}), {2}: (9, {})} | custom-call | flops 4026531840 | bytes 8388608 | tf_op jit(solution)/shard_map/weight_grads/pallas_call | solution.py:308
  259.2 9.3 %weight_grads.6 = (bf16[2,4096,256]{2,1,0:T(8,128)(2,1)}, bf16[2,4096,256]{2,1,0:T(8,128)(2,1)}, bf16[2,256,4096]{2,1,0:T(8,128)(2,1)}) custom-call(s32[1]{0:T(128)} %bitcast.at, bf16[4,1280,512]{2,1,0:T(8,128)(2,1)} %bitcast.52, bf16[1280,2048]{1,0:T(8,128)(2,1)} %bitcast.6.refs_4_.xp, ...), custom_call_target="tpu_custom_call", output_to_operand_aliasing={{0}: (7, {}), {1}: (8, {}), {2}: (9, {})} | custom-call | flops 4026531840 | bytes 8388608 | tf_op jit(solution)/shard_map/weight_grads/pallas_call | solution.py:308
  269.9 7.5 %all-to-all-start.6 = ((bf16[32,40,512]{2,1,0:T(8,128)(2,1)}), bf16[32,40,512]{2,1,0:T(8,128)(2,1)}, u32[]{:S(2)}, u32[]{:S(2)}) async-start(bf16[32,40,512]{2,1,0:T(8,128)(2,1)} %bitcast.62), calls=%async_computation.7 | async-start | bytes 2621440 | tf_op jit(solution)/shard_map/all_to_all | solution.py:164
  282.4 9.2 %weight_grads.7 = (bf16[2,4096,256]{2,1,0:T(8,128)(2,1)}, bf16[2,4096,256]{2,1,0:T(8,128)(2,1)}, bf16[2,256,4096]{2,1,0:T(8,128)(2,1)}) custom-call(s32[1]{0:T(128)} %bitcast.at, bf16[4,1280,512]{2,1,0:T(8,128)(2,1)} %bitcast.53, bf16[1280,2048]{1,0:T(8,128)(2,1)} %bitcast.6.refs_4_.xp, ...), custom_call_target="tpu_custom_call", output_to_operand_aliasing={{0}: (7, {}), {1}: (8, {}), {2}: (9, {})} | custom-call | flops 4026531840 | bytes 8388608 | tf_op jit(solution)/shard_map/weight_grads/pallas_call | solution.py:308
  292.2 6.6 %collective-permute-done.3 = f32[128,384]{1,0:T(8,128)S(1)} collective-permute-done((f32[128,384]{1,0:T(8,128)S(1)}, f32[128,384]{1,0:T(8,128)S(1)}, u32[]{:S(2)}, u32[]{:S(2)}) %collective-permute-start.3) | collective-permute-done | bytes 196640 | tf_op jit(solution)/shard_map/ppermute | solution.py:145
  298.9 14.4 %reduce-scatter.5.cloned.1.call-done = bf16[1,1280,256]{2,1,0:T(8,128)(2,1)} async-done(((bf16[4,1280,256]{2,1,0:T(8,128)(2,1)}), bf16[1,1280,256]{2,1,0:T(8,128)(2,1)}) %reduce-scatter.5.cloned.1.call-update) | async-done | bytes 655376 | tf_op jit(solution)/shard_map/reduce_scatter | solution.py:307
  313.3 7.6 %all-to-all-start.7 = ((bf16[32,40,256]{2,1,0:T(8,128)(2,1)}), bf16[32,40,256]{2,1,0:T(8,128)(2,1)S(1)}, u32[]{:S(2)}, u32[]{:S(2)}) async-start(bf16[32,40,256]{2,1,0:T(8,128)(2,1)} %bitcast.63), calls=%async_computation.9 | async-start | bytes 1310720 | tf_op jit(solution)/shard_map/all_to_all | solution.py:164
  323.5 10.4 %all-to-all-done.7 = bf16[32,40,256]{2,1,0:T(8,128)(2,1)S(1)} async-done(((bf16[32,40,256]{2,1,0:T(8,128)(2,1)}), bf16[32,40,256]{2,1,0:T(8,128)(2,1)S(1)}, u32[]{:S(2)}, u32[]{:S(2)}) %all-to-all-start.7) | async-done | bytes 655392 | tf_op jit(solution)/shard_map/all_to_all | solution.py:164
  (87 shorter events, 44.2 us)
Async XLA Ops:
  8.6 12.6 %copy-start.5 = (bf16[128,1024]{1,0:T(8,128)(2,1)S(1)}, bf16[128,1024]{1,0:T(8,128)(2,1)}, u32[]{:S(2)}) copy-start(bf16[128,1024]{1,0:T(8,128)(2,1)} %param.7) | copy-start | bytes 786436
  8.6 12.6 %copy-start.4 = (bf16[128,1024]{1,0:T(8,128)(2,1)S(1)}, bf16[128,1024]{1,0:T(8,128)(2,1)}, u32[]{:S(2)}) copy-start(bf16[128,1024]{1,0:T(8,128)(2,1)} %param.8) | copy-start | bytes 786436
  11.5 29.4 %all-to-all-start = ((bf16[32,40,512]{2,1,0:T(8,128)(2,1)}), bf16[32,40,512]{2,1,0:T(8,128)(2,1)S(1)}, u32[]{:S(2)}, u32[]{:S(2)}) async-start(bf16[32,40,512]{2,1,0:T(8,128)(2,1)} %bitcast.1), calls=%async_computation | async-start | bytes 2621440 | tf_op jit(solution)/shard_map/all_to_all | solution.py:164
  21.1 132.2 %all-gather.7.cloned.1.call-start = ((), (), s32[]{:S(2)}) async-start(), calls=%async_computation.13 | async-start | bytes 6553600 | tf_op jit(solution)/shard_map/all_gather | solution.py:178
  21.3 7.5 %collective-permute-start.2 = (bf16[128,768]{1,0:T(8,128)(2,1)S(1)}, bf16[128,768]{1,0:T(8,128)(2,1)S(1)}, u32[]{:S(2)}, u32[]{:S(2)}) collective-permute-start(bf16[128,768]{1,0:T(8,128)(2,1)S(1)} %pad_maximum_fusion.3), channel_id=1, source_target_pairs={{0,1},{1,2},{2,3},{3,0},{4,5},{5,6},{6,7},{7,4},{8,9},{9,10},{10,1... | collective-permute-start | bytes 589832 | tf_op jit(solution)/shard_map/ppermute | solution.py:145
  22.6 11.5 %collective-permute-start.1 = (bf16[128,768]{1,0:T(8,128)(2,1)S(1)}, bf16[128,768]{1,0:T(8,128)(2,1)S(1)}, u32[]{:S(2)}, u32[]{:S(2)}) collective-permute-start(bf16[128,768]{1,0:T(8,128)(2,1)S(1)} %pad_maximum_fusion.3), channel_id=1, source_target_pairs={{0,2},{1,3},{2,0},{3,1},{4,6},{5,7},{6,4},{7,5},{8,10},{9,11},{10,... | collective-permute-start | bytes 589832 | tf_op jit(solution)/shard_map/ppermute | solution.py:145
  25.0 9.0 %collective-permute-start = (bf16[128,768]{1,0:T(8,128)(2,1)S(1)}, bf16[128,768]{1,0:T(8,128)(2,1)S(1)}, u32[]{:S(2)}, u32[]{:S(2)}) collective-permute-start(bf16[128,768]{1,0:T(8,128)(2,1)S(1)} %pad_maximum_fusion.3), channel_id=1, source_target_pairs={{0,3},{1,0},{2,1},{3,2},{4,7},{5,4},{6,5},{7,6},{8,11},{9,8},{10,9... | collective-permute-start | bytes 589832 | tf_op jit(solution)/shard_map/ppermute | solution.py:145
  42.0 31.0 %all-to-all-start.1 = ((bf16[32,40,768]{2,1,0:T(8,128)(2,1)}), bf16[32,40,768]{2,1,0:T(8,128)(2,1)S(1)}, u32[]{:S(2)}, u32[]{:S(2)}) async-start(bf16[32,40,768]{2,1,0:T(8,128)(2,1)} %bitcast.59), calls=%async_computation.1 | async-start | bytes 3932160 | tf_op jit(solution)/shard_map/all_to_all | solution.py:164
  46.1 132.0 %all-gather.5.cloned.1.call-start = ((), (), s32[]{:S(2)}) async-start(), calls=%async_computation.12 | async-start | bytes 9830400 | tf_op jit(solution)/shard_map/all_gather | solution.py:181
  73.1 1.3 copy-start.1
  74.4 70.0 %all-to-all-start.2 = ((bf16[32,40,2048]{2,1,0:T(8,128)(2,1)}), bf16[32,40,2048]{2,1,0:T(8,128)(2,1)}, u32[]{:S(2)}, u32[]{:S(2)}) async-start(bf16[32,40,2048]{2,1,0:T(8,128)(2,1)} %bitcast.54), calls=%async_computation.2 | async-start | bytes 10485760 | tf_op jit(solution)/shard_map/all_to_all | solution.py:164
  144.3 43.3 %all-to-all-start.3 = ((bf16[32,40,1024]{2,1,0:T(8,128)(2,1)}), bf16[32,40,1024]{2,1,0:T(8,128)(2,1)S(1)}, u32[]{:S(2)}, u32[]{:S(2)}) async-start(bf16[32,40,1024]{2,1,0:T(8,128)(2,1)} %bitcast.56), calls=%async_computation.3 | async-start | bytes 5242880 | tf_op jit(solution)/shard_map/all_to_all | solution.py:164
  153.2 116.6 %reduce-scatter.3.cloned.1.call-start = ((), (), s32[]{:S(2)}) async-start(), calls=%async_computation.10 | async-start | bytes 6553600 | tf_op jit(solution)/shard_map/reduce_scatter | solution.py:286
  187.6 1.6 copy-start
  211.0 15.2 %all-to-all-start.5 = ((f32[32,1,40]{2,1,0:T(1,128)}), f32[32,1,40]{2,1,0:T(1,128)S(1)}, u32[]{:S(2)}, u32[]{:S(2)}) async-start(f32[32,1,40]{2,1,0:T(1,128)} %bitcast.14), calls=%async_computation.6 | async-start | bytes 32768 | tf_op jit(solution)/shard_map/all_to_all | solution.py:285
  226.2 43.5 %all-to-all-start.4 = ((bf16[32,40,1024]{2,1,0:T(8,128)(2,1)}), bf16[32,40,1024]{2,1,0:T(8,128)(2,1)S(1)}, u32[]{:S(2)}, u32[]{:S(2)}) async-start(bf16[32,40,1024]{2,1,0:T(8,128)(2,1)} %bitcast.57), calls=%async_computation.5 | async-start | bytes 5242880 | tf_op jit(solution)/shard_map/all_to_all | solution.py:164
  233.7 79.6 %reduce-scatter.5.cloned.1.call-start = ((), (), s32[]{:S(2)}) async-start(), calls=%async_computation.11 | async-start | bytes 3276800 | tf_op jit(solution)/shard_map/reduce_scatter | solution.py:307
  269.8 8.3 %copy-start.6 = (s32[128,8]{0,1:T(8,128)S(1)}, s32[128,8]{0,1:T(8,128)}, u32[]{:S(2)}) copy-start(s32[128,8]{0,1:T(8,128)} %param.9) | copy-start | bytes 12292
  269.9 29.0 %all-to-all-start.6 = ((bf16[32,40,512]{2,1,0:T(8,128)(2,1)}), bf16[32,40,512]{2,1,0:T(8,128)(2,1)}, u32[]{:S(2)}, u32[]{:S(2)}) async-start(bf16[32,40,512]{2,1,0:T(8,128)(2,1)} %bitcast.62), calls=%async_computation.7 | async-start | bytes 2621440 | tf_op jit(solution)/shard_map/all_to_all | solution.py:164
  278.9 12.7 %collective-permute-start.5 = (f32[128,384]{1,0:T(8,128)S(1)}, f32[128,384]{1,0:T(8,128)S(1)}, u32[]{:S(2)}, u32[]{:S(2)}) collective-permute-start(f32[128,384]{1,0:T(8,128)S(1)} %get-tuple-element.106), channel_id=1, source_target_pairs={{0,3},{1,0},{2,1},{3,2},{4,7},{5,4},{6,5},{7,6},{8,11},{9,8},{10,9... | collective-permute-start | bytes 589832 | tf_op jit(solution)/shard_map/ppermute | solution.py:145
  280.1 12.0 %collective-permute-start.4 = (f32[128,384]{1,0:T(8,128)S(1)}, f32[128,384]{1,0:T(8,128)S(1)}, u32[]{:S(2)}, u32[]{:S(2)}) collective-permute-start(f32[128,384]{1,0:T(8,128)S(1)} %get-tuple-element.105), channel_id=1, source_target_pairs={{0,2},{1,3},{2,0},{3,1},{4,6},{5,7},{6,4},{7,5},{8,10},{9,11},{10,... | collective-permute-start | bytes 589832 | tf_op jit(solution)/shard_map/ppermute | solution.py:145
  281.9 39.0 %copy-start.7 = (bf16[128,8]{0,1:T(8,128)(2,1)S(1)}, bf16[128,8]{0,1:T(8,128)(2,1)}, u32[]{:S(2)}) copy-start(bf16[128,8]{0,1:T(8,128)(2,1)} %param.10) | copy-start | bytes 6148
  281.9 16.9 %collective-permute-start.3 = (f32[128,384]{1,0:T(8,128)S(1)}, f32[128,384]{1,0:T(8,128)S(1)}, u32[]{:S(2)}, u32[]{:S(2)}) collective-permute-start(f32[128,384]{1,0:T(8,128)S(1)} %get-tuple-element.104), channel_id=1, source_target_pairs={{0,1},{1,2},{2,3},{3,0},{4,5},{5,6},{6,7},{7,4},{8,9},{9,10},{10,1... | collective-permute-start | bytes 589832 | tf_op jit(solution)/shard_map/ppermute | solution.py:145
  313.3 20.6 %all-to-all-start.7 = ((bf16[32,40,256]{2,1,0:T(8,128)(2,1)}), bf16[32,40,256]{2,1,0:T(8,128)(2,1)S(1)}, u32[]{:S(2)}, u32[]{:S(2)}) async-start(bf16[32,40,256]{2,1,0:T(8,128)(2,1)} %bitcast.63), calls=%async_computation.9 | async-start | bytes 1310720 | tf_op jit(solution)/shard_map/all_to_all | solution.py:164
  (2 other events, 2.1 us)
Sparse Core Ops, SparseCore 0:
  42.1 54.4 all-gather.6
  98.8 79.1 all-gather.4
  209.2 56.3 reduce-scatter.2
  270.0 43.2 reduce-scatter.4
